TPU v7x, 128 devices: a whole 4x4x4 slice. The times are simulated.
128 devices in a mesh: dp: 16 (over y_lo, z, core), fsdp: 8 (over y_hi, x).
Axes of the slice: x: 4, y: 4 (y_hi: 2, y_lo: 2; y = y_hi * 2 + y_lo), z: 4, core: 2. Of those that a mesh axis runs over, the one named last changes fastest.
Arguments:
- tokens: bfloat16 [49152, 1024], P(('dp', 'fsdp')), may hold values from -6 to 6
- norm1_gain: bfloat16 [1024], P('fsdp'), may hold values from 0.25 to 1.75
- norm1_bias: bfloat16 [1024], P('fsdp'), may hold values from -1.75 to 1.75
- qkv_weight: bfloat16 [1024, 3072], P('fsdp'), may hold values from -0.1875 to 0.1875
- query_bias: bfloat16 [1024], P('fsdp'), may hold values from -1.75 to 1.75
- value_bias: bfloat16 [1024], P('fsdp'), may hold values from -1.25 to 1.25
- out_weight: bfloat16 [1024, 1024], P('fsdp'), may hold values from -0.75 to 0.75
- out_bias: bfloat16 [1024], P('fsdp'), may hold values from -1.25 to 1.25
- norm2_gain: bfloat16 [1024], P('fsdp'), may hold values from 0.25 to 1.75
- norm2_bias: bfloat16 [1024], P('fsdp'), may hold values from -1.75 to 1.75
- fc1_weight: bfloat16 [1024, 4096], P('fsdp'), may hold values from -0.1875 to 0.1875
- fc1_bias: bfloat16 [4096], P('fsdp'), may hold values from -1.25 to 1.25
- fc2_weight: bfloat16 [4096, 1024], P('fsdp'), may hold values from -0.09375 to 0.09375
- fc2_bias: bfloat16 [1024], P('fsdp'), may hold values from -1.25 to 1.25
- cotangent: bfloat16 [49152, 1024], P(('dp', 'fsdp')), may hold values from -6 to 6
- group_of: int32 [16], replicated, may hold values from 0 to 1, as said below
- keep_mask: int32 [49152], P(('dp', 'fsdp')), may hold values from 0 to 1, as said below
- group_tokens: int32 [2], replicated, may hold values from 1000 to 4999
Outputs:
- block_out: bfloat16 [49152, 1024], P(('dp', 'fsdp'))
- input_grad: bfloat16 [49152, 1024], P(('dp', 'fsdp'))
- grad_norm1_gain: float32 [1024], P('fsdp')
- grad_norm1_bias: float32 [1024], P('fsdp')
- grad_qkv_weight: float32 [1024, 3072], P('fsdp')
- grad_query_bias: float32 [1024], P('fsdp')
- grad_value_bias: float32 [1024], P('fsdp')
- grad_out_weight: float32 [1024, 1024], P('fsdp')
- grad_out_bias: float32 [1024], P('fsdp')
- grad_norm2_gain: float32 [1024], P('fsdp')
- grad_norm2_bias: float32 [1024], P('fsdp')
- grad_fc1_weight: float32 [1024, 4096], P('fsdp')
- grad_fc1_bias: float32 [4096], P('fsdp')
- grad_fc2_weight: float32 [4096, 1024], P('fsdp')
- grad_fc2_bias: float32 [1024], P('fsdp')
Inputs may be any that keep to these rules, and one draw needn't show every extreme that they name: `group_of`: exactly 6 indices of dp hold 1; each device of such an index holds 2 images in slots of 192 rows, every other device 6 images in slots of 64 rows. `keep_mask`: in every image slot the kept tokens are the first n slots and the rest are 0; n is 25 to 50 for a slot of 64 rows and 72 to 145 for a slot of 192 rows, and every device has an image that keeps the most.
All inputs are finite; a program needn't handle non-finite values.
Results may differ from a plain program's by a relative error of at most 0.018.
Values may be sent and summed in bfloat16 or wider, within the bound.
No kernel may reach another device: no remote copies, remote signals or barrier semaphores. Data moves between devices by JAX's collectives and lax.ppermute only.
A program may use at most 256 MiB of HBM per device.

v0:
```python
import functools

import jax
import jax.numpy as jnp
from jax import lax
from jax.experimental import pallas as pl
from jax.experimental.pallas import tpu as pltpu
from jax.sharding import PartitionSpec as P

HEAD_DIM = 64
SLOT_S = 64
SLOT_L = 192
SPAN = 192
MOST_S = 50
USED = SPAN // SLOT_S * MOST_S
BLOCK = 160
EPS = 1e-06
AXES = ("dp", "fsdp")
BF = jnp.bfloat16
F32 = jnp.float32

Z_GROUPS = [[lo * 8 + 2 * z + c for z in range(4)] for lo in range(2) for c in range(2)]
SLICE_GROUPS = [[lo * 8 + 2 * z + c for z in range(4) for lo in range(2)] for c in range(2)]
X_GROUPS = [[0, 1, 2, 3], [4, 5, 6, 7]]


def place(linear):
    dp, fs = divmod(linear, 8)
    return fs % 4, (fs // 4) * 2 + dp // 8, (dp // 2) % 4, dp % 2


def linear_of(x, y, z, c):
    x, y, z = x % 4, y % 4, z % 4
    return (((y % 2) * 4 + z) * 2 + c) * 8 + (y // 2) * 4 + x


def permute(value, move):
    return lax.ppermute(
        value, AXES, [(l, linear_of(*move(*place(l)))) for l in range(128)]
    )


def ring_move(axis):
    def move(x, y, z, c):
        s = 1 - 2 * c
        return (x + s * (axis == "x"), y + s * (axis == "y"), z + s * (axis == "z"), c)

    return move


def shift(axis, s):
    def move(x, y, z, c):
        return (x + s * (axis == "x"), y + s * (axis == "y"), z + s * (axis == "z"), c)

    return move


HOPS = (1, 2, 3)


def swap_core(x, y, z, c):
    return x, y, z, 1 - c


def flip_hi(x, y, z, c):
    return x, 3 - y, z, c


def flip_lo(x, y, z, c):
    return x, y ^ 1, z, c


class Where:
    def __init__(self):
        dp, fs = lax.axis_index("dp"), lax.axis_index("fsdp")
        self.dp, self.fs = dp, fs
        self.c = dp % 2
        self.z = (dp // 2) % 4
        self.lo = dp // 8
        self.x = fs % 4
        self.hi = fs // 4
        self.y = self.hi * 2 + self.lo
        self.sign = 1 - 2 * self.c

    def along(self, axis):
        return {"x": self.x, "y": self.y, "z": self.z}[axis]

    def source(self, axis, step):
        return lax.rem(self.along(axis) - self.sign * step + 8, 4)

    def make_table(self):
        self.table = jnp.stack([self.c, self.z, self.lo, self.hi, self.x, self.y]).astype(jnp.int32)


C, Z, LO, HI, X, Y = range(6)


def source_in(table, at, step):
    return lax.rem(table[at] - (1 - 2 * table[C]) * step + 8, 4)


def place_in(table, at, r):
    return lax.rem(table[at] + r + 4, 4)


def pick(stacked, index, axis=0):
    return lax.dynamic_index_in_dim(stacked, index, axis, keepdims=False)


def ring_gather(here, value, axis, buffer, put):
    for step in range(4):
        if step:
            value = permute(value, ring_move(axis))
        buffer = put(buffer, value, here.source(axis, step))
    return buffer


def ring_reduce(here, axis, term):
    total = term(here.source(axis, 1))
    for step in range(2, 5):
        total = permute(total, ring_move(axis))
        total = (total.astype(F32) + term(here.source(axis, step)).astype(F32)).astype(BF)
    return total


def ring_blocks(value, axis):
    blocks = [value]
    for _ in range(3):
        blocks.append(permute(blocks[-1], ring_move(axis)))
    return blocks


def exchange(blocks, axis):
    return [blocks[0]] + [permute(blocks[r], shift(axis, r)) for r in HOPS]


ANY = pl.BlockSpec(memory_space=pl.ANY)
SMEM = pl.BlockSpec(memory_space=pltpu.SMEM)
VMEM = pl.BlockSpec(memory_space=pltpu.VMEM)


TOKEN = jax.ShapeDtypeStruct((8, 128), jnp.float32)
TOKEN_SPEC = pl.BlockSpec((8, 128), lambda i: (0, 0))


def in_hbm(value):
    return pltpu.with_memory_space_constraint(value, pltpu.HBM)


def kernel_call(
    kernel,
    name,
    out_shape,
    in_specs,
    us=1,
    vmem=16 << 20,
    pinned=(),
    pinned_out=(),
    late=(),
    **kwargs,
):
    count = len(in_specs)
    if pinned_out:
        shapes = out_shape if isinstance(out_shape, list) else [out_shape]
        shapes = [
            pltpu.HBM(s.shape, s.dtype) if n in pinned_out else s for n, s in enumerate(shapes)
        ]
        out_shape = shapes if isinstance(out_shape, list) else shapes[0]

    def body(*refs):
        kernel(*refs[:count], *refs[count + len(late) :])

    call = pl.pallas_call(
        body,
        out_shape=out_shape,
        in_specs=list(in_specs) + [ANY] * len(late),
        name=name,
        compiler_params=pltpu.CompilerParams(vmem_limit_bytes=vmem),
        cost_estimate=pl.CostEstimate(
            flops=int(us * 0.25 * 1.15e9), bytes_accessed=1 << 16, transcendentals=0
        ),
        **kwargs,
    )

    def run(*args):
        return call(
            *(in_hbm(a) if n in pinned else a for n, a in enumerate(args)),
            *(in_hbm(a) if a.size > 1 << 16 else a for a in late),
        )

    return run


def struct(shape, dtype):
    return jax.ShapeDtypeStruct(shape, dtype)


def assemble(here, name, parts, shape, target, source=lambda ref: ref, late=()):
    def kernel(table, *refs):
        ins, out, sems = refs[: len(parts)], refs[len(parts)], refs[len(parts) + 1]
        copies = [
            pltpu.make_async_copy(source(ins[n]), target(out, table, n), sems.at[n])
            for n in range(len(parts))
        ]
        for copy in copies:
            copy.start()
        for copy in copies:
            copy.wait()

    return kernel_call(
        kernel,
        name,
        struct(shape, BF),
        in_specs=[SMEM] + [ANY] * len(parts),
        us=2.5,
        pinned=range(1, 1 + len(parts)),
        late=late,
        out_specs=VMEM,
        scratch_shapes=[pltpu.SemaphoreType.DMA((len(parts),))],
    )(here.table, *parts)


def lane_halves(c, left, right):
    first = lax.broadcasted_iota(jnp.int32, left.shape, 1) < 64
    low = jnp.where(first, left, pltpu.roll(right, 64, 1))
    high = jnp.where(first, pltpu.roll(left, 64, 1), right)
    return jnp.where(c == 0, low, high)


def prepare_kernel(place_ref, qkv, fc1, fc2, out, *refs):
    vectors, (qkv_rep, fc1_part, fc2_half, out_half) = refs[:9], refs[9:]
    c, z, lo = place_ref[0], place_ref[1], place_ref[2]
    rows = pl.ds(pl.multiple_of(z * 32, 32), 32)
    for g in range(12):
        left = qkv[rows, g * 256 : g * 256 + 128].astype(F32)
        right = qkv[rows, g * 256 + 128 : g * 256 + 256].astype(F32)
        half = lane_halves(c, left, right).astype(BF)
        for d in range(8):
            qkv_rep[d, :, g * 128 : (g + 1) * 128] = half
    packed = [ref[...].astype(F32).reshape(-1, 128) for ref in vectors]
    packed = jnp.concatenate(packed + [jnp.zeros((20, 128), F32)]).astype(BF)
    for d in range(8):
        qkv_rep[d, :, 1536:] = packed
    out_half[...] = out[pl.ds(pl.multiple_of(c * 64, 64), 64), :]
    rows = pl.ds(pl.multiple_of(lo * 64, 64), 64)
    for f in range(8):
        half = jnp.where(
            c == 0, fc1[rows, f * 512 : f * 512 + 256], fc1[rows, f * 512 + 256 : (f + 1) * 512]
        )
        fc1_part[:, f * 256 : (f + 1) * 256] = half
    fc2_half[...] = fc2[pl.ds(pl.multiple_of(c * 256, 256), 256), :]


def row_choice(group):
    i = lax.broadcasted_iota(jnp.int32, (BLOCK, SPAN), 0)
    j = lax.broadcasted_iota(jnp.int32, (BLOCK, SPAN), 1)
    slot = (i >= MOST_S).astype(jnp.int32) + (i >= 2 * MOST_S).astype(jnp.int32)
    source = jnp.where(group == 1, i, i + slot * (SLOT_S - MOST_S))
    return jnp.where((j == source) & (i < USED), 1.0, 0.0)


def chosen_rows(group):
    j = lax.broadcasted_iota(jnp.int32, (SPAN, 1), 0)
    slot = (j >= SLOT_S).astype(jnp.int32) + (j >= 2 * SLOT_S).astype(jnp.int32)
    place = jnp.where(group == 1, j, j - slot * SLOT_S)
    return place < jnp.where(group == 1, USED, MOST_S)


def image_of(group, shape, axis):
    i = lax.broadcasted_iota(jnp.int32, shape, axis)
    slot = (i >= MOST_S).astype(jnp.int32) + (i >= 2 * MOST_S).astype(jnp.int32)
    return jnp.where(group == 1, 0, slot)


def compact_kernel(
    groups, shares, tokens, tokens_other, cot, cot_other, keep, keep_other, rows, cots, d_branch, column, blocked
):
    step = pl.program_id(0)
    own = step < 2
    group = groups[step // 2]
    choice = row_choice(group)
    low = choice.astype(BF)
    kept = jnp.where(own, keep[...], keep_other[...]).astype(F32)
    rows[...] = dot(low, jnp.where(own, tokens[...], tokens_other[...])).astype(BF)
    chosen = dot(low, jnp.where(own, cot[...], cot_other[...]))
    cots[...] = chosen.astype(BF)
    mask = jnp.sum(choice * kept, axis=-1, keepdims=True)
    column[...] = mask
    d_branch[...] = (mask * (chosen * shares[step // 2])).astype(BF)
    across = dot_nt(jnp.broadcast_to(kept, (16, SPAN)).astype(BF), low)[:1]
    same = image_of(group, (BLOCK, BLOCK), 0) == image_of(group, (BLOCK, BLOCK), 1)
    blocked[...] = jnp.where(same & (across > 0.5), 0.0, -1e30)


def compact(groups, shares, tokens, tokens_other, cot, cot_other, keep, keep_other):
    def mine(shape, rows):
        return pl.BlockSpec(shape, lambda i: (jnp.minimum(i, 1),) + (0,) * (len(shape) - 1))

    def theirs(shape, rows):
        return pl.BlockSpec(shape, lambda i: (jnp.maximum(i - 2, 0),) + (0,) * (len(shape) - 1))

    row = (SPAN, 1024)
    flag = (None, 1, SPAN)
    tile = pl.BlockSpec((BLOCK, 1024), lambda i: (i, 0))
    return kernel_call(
        compact_kernel,
        "compact",
        [struct((4 * BLOCK, 1024), BF)] * 3
        + [struct((4 * BLOCK, 1), F32), struct((4, BLOCK, BLOCK), F32)],
        us=5,
        grid=(4,),
        in_specs=[
            SMEM,
            SMEM,
            mine(row, 2),
            theirs(row, 2),
            mine(row, 2),
            theirs(row, 2),
            mine(flag, 2),
            theirs(flag, 2),
        ],
        out_specs=[
            tile,
            tile,
            tile,
            pl.BlockSpec((BLOCK, 1), lambda i: (i, 0)),
            pl.BlockSpec((None, BLOCK, BLOCK), lambda i: (i, 0, 0)),
        ],
    )(
        groups,
        shares,
        tokens,
        tokens_other,
        cot,
        cot_other,
        keep.reshape(2, 1, SPAN),
        keep_other.reshape(2, 1, SPAN),
    )


def spread(group, values, rest):
    back = dot_tn(row_choice(group).astype(BF), values)
    return jnp.where(chosen_rows(group), back, rest.astype(F32)).astype(BF)


def block_out_kernel(groups, branch, sent, middle, column, shift, tokens, out):
    total = branch[...] + sent[...].astype(F32) + shift[...]
    values = (middle[...] + column[...] * total).astype(BF)
    out[...] = spread(groups[0], values, tokens[...])


def block_out_layer(groups, branch, sent, middle, column, shift, tokens):
    tile = pl.BlockSpec((BLOCK, 1024), lambda i: (i, 0))
    span = pl.BlockSpec((SPAN, 1024), lambda i: (i, 0))
    return kernel_call(
        lambda *refs: block_out_kernel(*refs[:-1]),
        "block_out",
        [struct(tokens.shape, BF), TOKEN],
        us=4,
        grid=(2,),
        in_specs=[
            SMEM,
            tile,
            tile,
            tile,
            pl.BlockSpec((BLOCK, 1), lambda i: (i, 0)),
            pl.BlockSpec((1, 1024), lambda i: (0, 0)),
            span,
        ],
        out_specs=[span, TOKEN_SPEC],
    )(groups, branch, sent, middle, column, shift, tokens)


def vectors_kernel(place_ref, packed, *outs):
    c = place_ref[0]
    rows = [packed[f].astype(F32) for f in range(8)]

    def row(f, k):
        return rows[f][k : k + 1, :]

    for out, k in zip(outs[:6], (0, 1, 4, 5, 6, 7)):
        for f in range(8):
            out[:, f * 128 : (f + 1) * 128] = row(f, k)
    for out, k in zip(outs[6:8], (2, 3)):
        for p in range(4):
            out[:, p * 128 : (p + 1) * 128] = lane_halves(c, row(2 * p, k), row(2 * p + 1, k))
    for f in range(8):
        for j in range(2):
            at = f * 256 + j * 128
            outs[8][:, at : at + 128] = jnp.where(c == 0, row(f, 8 + j), row(f, 10 + j))


def vector_terms_kernel(place_ref, input_sums, packed_sums, middle_sums, fc1_sums, out):
    c = place_ref[0]
    first = lax.broadcasted_iota(jnp.int32, (1, 128), 1) < 64
    zero = jnp.zeros((1, 128), F32)
    out[...] = jnp.zeros_like(out)
    whole = (
        (0, input_sums, 0),
        (1, input_sums, 1),
        (4, middle_sums, 2),
        (5, middle_sums, 0),
        (6, middle_sums, 1),
        (7, middle_sums, 3),
    )
    for f in range(8):
        for k, ref, r in whole:
            out[f, k : k + 1, :] = ref[r : r + 1, f * 128 : (f + 1) * 128]
        for j in range(4):
            at = f * 256 + (j % 2) * 128
            out[f, 8 + j : 9 + j, :] = jnp.where(c == j // 2, fc1_sums[:, at : at + 128], zero)
    for k, base in ((2, 0), (3, 1024)):
        for p in range(4):
            pair = packed_sums[:, base + p * 128 : base + (p + 1) * 128]
            turned = pltpu.roll(pair, 64, 1)
            for e in range(2):
                low = jnp.where(first, pair if e == 0 else turned, zero)
                high = jnp.where(first, zero, turned if e == 0 else pair)
                out[2 * p + e, k : k + 1, :] = jnp.where(c == 0, low, high)


def grad_fc2_kernel(left, right, out):
    terms = dot_tn(left[...], right[...]).astype(BF)
    for x in range(2):
        for z in range(4):
            at = (4 * x + z) * 64
            out[z, x] = terms[at : at + 64]


def grad_fc2_terms(hidden, d_branch, late):
    m = hidden.shape[0]
    return kernel_call(
        lambda *refs: grad_fc2_kernel(*refs[:-1]),
        "grad_fc2",
        [struct((4, 8, 64, 1024), BF), TOKEN],
        us=5,
        late=late,
        pinned_out=(0,),
        grid=(4,),
        in_specs=[
            pl.BlockSpec((m, 512), lambda i: (0, i)),
            pl.BlockSpec((m, 1024), lambda i: (0, 0)),
        ],
        out_specs=[
            pl.BlockSpec((4, 2, 64, 1024), lambda i: (0, i, 0, 0)),
            TOKEN_SPEC,
        ],
    )(hidden, d_branch)


def grad_fc1_kernel(table, left, right, *refs):
    outs = refs[:4]
    terms = dot_tn(left[...], right[...]).astype(BF)
    hi = lax.rem(pl.program_id(0), 2)
    for n, out in enumerate(outs):
        y = source_in(table, Y, n + 1)
        for lo in range(2):

            @pl.when(y == hi * 2 + lo)
            def _():
                for x in range(2):
                    at = (2 * x + lo) * 64
                    out[x] = terms[at : at + 64]


def grad_fc1_terms(here, normed, d_pre, late):
    m = normed.shape[0]
    return kernel_call(
        grad_fc1_kernel,
        "grad_fc1",
        [struct((4, 64, 2048), BF)] * 4 + [TOKEN],
        us=5,
        late=late,
        pinned_out=range(4),
        grid=(4,),
        in_specs=[
            SMEM,
            pl.BlockSpec((m, 256), lambda i: (0, lax.rem(i, 2) * 2 + i // 2)),
            pl.BlockSpec((m, 2048), lambda i: (0, 0)),
        ],
        out_specs=[pl.BlockSpec((2, 64, 2048), lambda i: (i // 2, 0, 0))] * 4 + [TOKEN_SPEC],
    )(here.table, normed, d_pre)


def grad_qkv_kernel(normed, d_packed, mixed, d_attended, out):
    qkv = dot_tn(normed[...], d_packed[...]).astype(BF)
    rest = dot_tn(mixed[...], d_attended[...])
    for f in range(2):
        parts = []
        for k in range(8):
            rows = rest[f * 64 + k * 8 : f * 64 + (k + 1) * 8]
            parts += [rows[:, :512], rows[:, 512:]]
        parts = jnp.concatenate(parts).astype(BF)
        for z in range(4):
            out[z, f, :, :1536] = qkv[f * 128 + z * 32 : f * 128 + (z + 1) * 32]
            out[z, f, :, 1536:] = parts[z * 32 : (z + 1) * 32]


def grad_qkv_terms(normed, d_packed, mixed, d_attended, late):
    m = normed.shape[0]
    return kernel_call(
        grad_qkv_kernel,
        "grad_qkv",
        struct((4, 8, 32, 2048), BF),
        us=5,
        late=late,
        pinned_out=(0,),
        grid=(4,),
        in_specs=[
            pl.BlockSpec((m, 256), lambda i: (0, i)),
            pl.BlockSpec((m, 1536), lambda i: (0, 0)),
            pl.BlockSpec((m, 128), lambda i: (0, i)),
            pl.BlockSpec((m, 1024), lambda i: (0, 0)),
        ],
        out_specs=pl.BlockSpec((4, 2, 32, 2048), lambda i: (0, i, 0, 0)),
    )(normed, d_packed, mixed, d_attended)


def total_of(refs):
    total = refs[0][...].astype(F32)
    for ref in refs[1:]:
        total = total + ref[...].astype(F32)
    return total


def sum_kernel(*refs):
    refs[-1][...] = total_of(refs[:-1]).astype(BF)


def sum_of(name, blocks, late=()):
    block = pl.BlockSpec((2,) + blocks[0].shape[1:], lambda i: (i, 0, 0))
    return kernel_call(
        lambda *refs: sum_kernel(*refs[:-1]),
        name,
        [struct(blocks[0].shape, BF), TOKEN],
        us=2,
        late=late,
        grid=(2,),
        in_specs=[block] * len(blocks),
        out_specs=[block, TOKEN_SPEC],
    )(*blocks)


def sum_first_kernel(blocks, out):
    out[...] = jnp.sum(blocks[...].astype(F32), axis=0).astype(BF)


def sum_first(name, blocks):
    k, r, n = blocks.shape
    return kernel_call(
        sum_first_kernel,
        name,
        struct((r, n), BF),
        us=1,
        grid=(1,),
        in_specs=[pl.BlockSpec((k, r, n), lambda i: (0, 0, 0))],
        out_specs=pl.BlockSpec((r, n), lambda i: (0, 0)),
    )(blocks)


def join_kernel(qkv, vectors, out):
    for f in range(8):
        out[f, :, :2048] = qkv[f]
        out[f, :16, 2048:] = vectors[f].astype(BF)
        out[f, 16:, 2048:] = jnp.zeros((16, 128), BF)


def join(qkv, vectors, late):
    return kernel_call(
        join_kernel,
        "join",
        struct((8, 32, 2176), BF),
        us=1,
        late=late,
        grid=(1,),
        in_specs=[
            pl.BlockSpec((8, 32, 2048), lambda i: (0, 0, 0)),
            pl.BlockSpec((8, 16, 128), lambda i: (0, 0, 0)),
        ],
        out_specs=pl.BlockSpec((8, 32, 2176), lambda i: (0, 0, 0)),
    )(qkv, vectors)


def split_kernel(table, blocks, kept, sent, vectors):
    total = jnp.sum(blocks[...].astype(F32), axis=0)
    half, n = kept.shape
    low, high = total[:half, :n], total[half:, :n]
    kept[...] = jnp.where(table[LO] == 0, low, high)
    sent[...] = jnp.where(table[LO] == 0, high, low).astype(BF)
    if total.shape[1] > n:
        vectors[...] = total[:16, n:]


def sum_and_halve(here, name, blocks, n):
    k, r, wide = blocks.shape
    half = pl.BlockSpec((r // 2, n), lambda i: (0, 0))
    kept, sent, vectors = kernel_call(
        split_kernel,
        name,
        [struct((r // 2, n), F32), struct((r // 2, n), BF), struct((16, 128), F32)],
        us=1,
        grid=(1,),
        in_specs=[SMEM, pl.BlockSpec((k, r, wide), lambda i: (0, 0, 0))],
        out_specs=[half, half, pl.BlockSpec((16, 128), lambda i: (0, 0))],
    )(here.table, blocks)
    return kept, permute(sent, flip_lo), vectors


def pack_kernel(qkv_kept, qkv_sent, fc2_kept, fc2_sent, fc1, vectors, packed):
    qkv = (qkv_kept[...] + qkv_sent[...].astype(F32)).astype(BF)
    fc2 = (fc2_kept[...] + fc2_sent[...].astype(F32)).astype(BF)
    fc1 = jnp.sum(fc1[...].astype(F32), axis=0).astype(BF)
    for d in range(8):
        packed[d, :16, :2048] = qkv
        packed[d, 16:32, :2048] = fc1
        packed[d, 32:, :1024] = fc2[:16]
        packed[d, 32:, 1024:2048] = fc2[16:]
        packed[d, :16, 2048:] = vectors[...].astype(BF)
        packed[d, 16:, 2048:] = jnp.zeros((32, 128), BF)


def unpack_kernel(place_ref, own, other, qkv, out, fc1, fc2, *vectors):
    c = place_ref[0]
    low = jnp.where(c == 0, own[...], other[...]).astype(F32)
    high = jnp.where(c == 0, other[...], own[...]).astype(F32)
    for k, half in enumerate((low, high)):
        out[k, :, :512] = half[:8, 1536:2048]
        out[k, :, 512:] = half[8:16, 1536:2048]
        fc2[k, :16] = half[32:, :1024]
        fc2[k, 16:] = half[32:, 1024:2048]
        for f in range(8):
            at = f * 512 + k * 256
            fc1[:, at : at + 256] = half[16:32, f * 256 : (f + 1) * 256]
    terms = low[:16, 2048:] + high[:16, 2048:]

    start = pl.program_id(0) == 0
    for k, ref in enumerate(vectors):
        rows = terms[k : k + ref.shape[0]]
        ref[...] = jnp.where(start, rows, ref[...] + rows)

    first = lax.broadcasted_iota(jnp.int32, (16, 128), 1) < 64
    for p in range(12):
        left, right = low[:16, p * 128 : (p + 1) * 128], high[:16, p * 128 : (p + 1) * 128]
        qkv[:, p * 256 : p * 256 + 128] = jnp.where(first, left, pltpu.roll(right, 64, 1))
        qkv[:, p * 256 + 128 : (p + 1) * 256] = jnp.where(first, pltpu.roll(left, 64, 1), right)


def all_to_all(value, axis, groups=None):
    return lax.all_to_all(value, axis, 0, 0, tiled=True, axis_index_groups=groups)


def add_over(value, *moves):
    for move in moves:
        value = value + permute(value, move)
    return value


RATE = 0.51
ERFC = (
    0.28791757708249816,
    0.28415126012743,
    0.2790719172776486,
    0.055036978129087616,
    0.35846874221749475,
    -0.3591518512954867,
    0.09450494290776956,
)


def hidden_kernel(rows, weight, shift, hidden, slope):
    for k in range(weight.shape[1] // 256):
        at = slice(k * 256, (k + 1) * 256)
        u = jnp.dot(rows[...], weight[:, at], preferred_element_type=F32) + shift[:, at]
        bell = jnp.exp(-0.5 * u * u)
        t = 1.0 / (1.0 + (RATE * 0.5**0.5) * jnp.abs(u))
        tail = jnp.full_like(u, 0.5 * ERFC[-1])
        for coefficient in ERFC[-2::-1]:
            tail = tail * t + 0.5 * coefficient
        tail = tail * t * bell
        area = jnp.where(u >= 0, 1.0 - tail, tail)
        hidden[:, at] = (u * area).astype(BF)
        slope[:, at] = (area + u * bell * 0.3989422804014327).astype(BF)


def hidden_layer(rows, weight, shift):
    m, k = rows.shape
    n = weight.shape[1]
    cols = 512
    out = pl.BlockSpec((m, cols), lambda i: (0, i))
    return kernel_call(
        hidden_kernel,
        "hidden_layer",
        [struct((m, n), BF)] * 2,
        us=11,
        grid=(n // cols,),
        in_specs=[
            pl.BlockSpec((m, k), lambda i: (0, 0)),
            pl.BlockSpec((k, cols), lambda i: (0, i)),
            pl.BlockSpec((1, cols), lambda i: (0, i)),
        ],
        out_specs=[out, out],
    )(rows, weight, shift)


def d_pre_kernel(grad, weight, slope, d_pre, total):
    back = dot_nt(grad[...], weight[...]) * slope[...].astype(F32)
    low = back.astype(BF)
    d_pre[...] = low
    total[...] = jnp.sum(low.astype(F32), axis=0, keepdims=True)


def hidden_back(grad, weight, slope, late):
    m, k = grad.shape
    n = weight.shape[0]
    cols = 256
    out = pl.BlockSpec((m, cols), lambda i: (0, i))
    return kernel_call(
        d_pre_kernel,
        "hidden_back",
        [struct((m, n), BF), struct((1, n), F32)],
        late=late,
        us=6,
        grid=(n // cols,),
        in_specs=[
            pl.BlockSpec((m, k), lambda i: (0, 0)),
            pl.BlockSpec((cols, k), lambda i: (i, 0)),
            out,
        ],
        out_specs=[out, pl.BlockSpec((1, cols), lambda i: (0, i))],
    )(grad, weight, slope)


def head_pair(packed, query_shift, value_shift, p):
    at = slice(p * 128, (p + 1) * 128)
    query = (packed[:, p * 128 : (p + 1) * 128] + query_shift[:, at]).astype(BF)
    key = packed[:, 512 + p * 128 : 512 + (p + 1) * 128].astype(BF)
    value = (packed[:, 1024 + p * 128 : 1024 + (p + 1) * 128] + value_shift[:, at]).astype(BF)
    return query, key, value


SCALE = HEAD_DIM ** (-0.5)


def stacked(pair, first):
    zero = jnp.zeros_like(pair)
    return jnp.concatenate([jnp.where(first, pair, zero), jnp.where(first, zero, pair)])


def merged(both, first):
    half = both.shape[0] // 2
    return jnp.where(first, both[:half], both[half:])


def softmax_of(queries, key, blocked):
    scores = dot_nt(queries, key) * SCALE + blocked
    exps = jnp.exp(scores - jnp.max(scores, axis=-1, keepdims=True))
    return exps * (1.0 / jnp.sum(exps, axis=-1, keepdims=True))


def attention_kernel(packed, query_shift, value_shift, blocked, mixed):
    first = lax.broadcasted_iota(jnp.int32, (BLOCK, 128), 1) < 64
    both = jnp.concatenate([blocked[...], blocked[...]])
    for p in range(4):
        query, key, value = head_pair(packed, query_shift, value_shift, p)
        probs = softmax_of(stacked(query, first), key, both)
        parts = dot(probs.astype(BF), value)
        mixed[:, p * 128 : (p + 1) * 128] = merged(parts, first).astype(BF)


def attention(packed, query_shift, value_shift, blocked, late):
    rows = packed.shape[0]
    shift = pl.BlockSpec((1, 512), lambda i: (0, 0))
    return kernel_call(
        lambda *refs: attention_kernel(*refs[:-1]),
        "attention",
        [struct((rows, 512), BF), TOKEN],
        us=5,
        late=late,
        grid=(rows // BLOCK,),
        in_specs=[
            pl.BlockSpec((BLOCK, 1536), lambda i: (i, 0)),
            shift,
            shift,
            pl.BlockSpec((None, BLOCK, BLOCK), lambda i: (i, 0, 0)),
        ],
        out_specs=[pl.BlockSpec((BLOCK, 512), lambda i: (i, 0)), TOKEN_SPEC],
    )(packed, query_shift, value_shift, blocked)


def attention_back_kernel(packed, query_shift, value_shift, blocked, d_mixed, d_packed, total):
    first = lax.broadcasted_iota(jnp.int32, (BLOCK, 128), 1) < 64

    @pl.when(pl.program_id(0) == 0)
    def _():
        total[...] = jnp.zeros_like(total)

    both = jnp.concatenate([blocked[...], blocked[...]])
    for p in range(4):
        query, key, value = head_pair(packed, query_shift, value_shift, p)
        queries = stacked(query, first)
        grads = stacked(d_mixed[:, p * 128 : (p + 1) * 128], first)
        probs = softmax_of(queries, key, both)
        d_probs = dot_nt(grads, value)
        d_scores = probs * (d_probs - jnp.sum(probs * d_probs, axis=-1, keepdims=True))
        d_scores = d_scores.astype(BF)
        parts = (
            merged(dot(d_scores, key), first) * SCALE,
            dot_tn(d_scores, queries) * SCALE,
            dot_tn(probs.astype(BF), grads),
        )
        for k, part in enumerate(parts):
            at = slice(k * 512 + p * 128, k * 512 + (p + 1) * 128)
            low = part.astype(BF)
            d_packed[:, at] = low
            total[:, at] += jnp.sum(low.astype(F32), axis=0, keepdims=True)


def attention_back(packed, query_shift, value_shift, blocked, d_mixed, late):
    rows = packed.shape[0]
    shift = pl.BlockSpec((1, 512), lambda i: (0, 0))
    return kernel_call(
        attention_back_kernel,
        "attention_back",
        [struct((rows, 1536), BF), struct((1, 1536), F32)],
        us=16,
        late=late,
        grid=(rows // BLOCK,),
        in_specs=[
            pl.BlockSpec((BLOCK, 1536), lambda i: (i, 0)),
            shift,
            shift,
            pl.BlockSpec((None, BLOCK, BLOCK), lambda i: (i, 0, 0)),
            pl.BlockSpec((BLOCK, 512), lambda i: (i, 0)),
        ],
        out_specs=[
            pl.BlockSpec((BLOCK, 1536), lambda i: (i, 0)),
            pl.BlockSpec((1, 1536), lambda i: (0, 0)),
        ],
    )(packed, query_shift, value_shift, blocked, d_mixed)


def dot(left, right):
    return jnp.dot(left, right, preferred_element_type=F32)


def dot_nt(left, right):
    return lax.dot_general(left, right, (((1,), (1,)), ((), ())), preferred_element_type=F32)


def dot_tn(left, right):
    return lax.dot_general(left, right, (((0,), (0,)), ((), ())), preferred_element_type=F32)


def normalize(values):
    center = values - jnp.mean(values, axis=-1, keepdims=True)
    rstd = lax.rsqrt(jnp.mean(center * center, axis=-1, keepdims=True) + EPS)
    return center * rstd, rstd


def normalize_back(grad, yhat, rstd, gain):
    t = grad * gain
    return rstd * (
        t
        - jnp.mean(t, axis=-1, keepdims=True)
        - yhat * jnp.mean(t * yhat, axis=-1, keepdims=True)
    )


TILE = 160


def middle_kernel(part, other, tokens, keep, shift, gain, bias, middle, normed):
    attended = part[...].astype(F32) + other[...].astype(F32) + shift[...]
    rows = tokens[...].astype(F32) + keep[...] * attended
    middle[...] = rows
    yhat, _ = normalize(rows)
    normed[...] = (yhat * gain[...] + bias[...]).astype(BF)


def row_specs(count, width=1024):
    half = count // 2
    return (
        pl.BlockSpec((TILE, width), lambda i: (i, 0)),
        pl.BlockSpec((TILE, width), lambda i: (lax.rem(i + half, count), 0)),
        pl.BlockSpec((TILE, 1), lambda i: (i, 0)),
        pl.BlockSpec((1, width), lambda i: (0, 0)),
    )


def middle_layer(part, other, tokens, keep, shift, gain, bias):
    rows = part.shape[0]
    tile, swapped, column, vector = row_specs(rows // TILE)
    return kernel_call(
        middle_kernel,
        "middle_layer",
        [struct((rows, 1024), F32), struct((rows, 1024), BF)],
        us=6,
        pinned_out=(0,),
        grid=(rows // TILE,),
        in_specs=[tile, swapped, tile, column, vector, vector, vector],
        out_specs=[tile, tile],
    )(part, other, tokens, keep, shift, gain, bias)


def middle_back_kernel(shares, part, other, middle, cot, keep, gain, d_middle, d_attended, sums):
    step = pl.program_id(0)
    grad = part[...].astype(F32) + other[...].astype(F32)
    yhat, rstd = normalize(middle[...])
    incoming = cot[...].astype(F32) * shares[step // (pl.num_programs(0) // 2)]
    d_rows = incoming + normalize_back(grad, yhat, rstd, gain[...])
    d_middle[...] = d_rows
    low = (keep[...] * d_rows).astype(BF)
    d_attended[...] = low
    branch = (keep[...] * incoming).astype(BF)

    @pl.when(step == 0)
    def _():
        sums[...] = jnp.zeros_like(sums)

    @pl.when(step < pl.num_programs(0) // 2)
    def _():
        for k, v in enumerate((grad * yhat, grad, low.astype(F32), branch.astype(F32))):
            sums[k : k + 1, :] += jnp.sum(v, axis=0, keepdims=True)


def middle_back(shares, part, other, middle, cot, keep, gain, late):
    rows = part.shape[0]
    tile, swapped, column, vector = row_specs(rows // TILE)
    return kernel_call(
        middle_back_kernel,
        "middle_back",
        [struct((rows, 1024), F32), struct((rows, 1024), BF), struct((8, 1024), F32)],
        us=7,
        late=late,
        pinned=(3, 4),
        grid=(rows // TILE,),
        in_specs=[SMEM, tile, swapped, tile, tile, column, vector],
        out_specs=[tile, tile, pl.BlockSpec((8, 1024), lambda i: (0, 0))],
    )(shares, part, other, middle, cot, keep, gain)


def input_back_kernel(groups, shares, part, other, rows, d_middle, gain, cot, grad_rows, sums):
    grad = part[...].astype(F32) + other[...].astype(F32)
    yhat, rstd = normalize(rows[...].astype(F32))
    values = (d_middle[...] + normalize_back(grad, yhat, rstd, gain[...])).astype(BF)
    rest = (cot[...].astype(F32) * shares[0]).astype(BF)
    grad_rows[...] = spread(groups[0], values, rest)

    @pl.when(pl.program_id(0) == 0)
    def _():
        sums[...] = jnp.zeros_like(sums)

    for k, v in enumerate((grad * yhat, grad)):
        sums[k : k + 1, :] += jnp.sum(v, axis=0, keepdims=True)


def input_back(groups, shares, part, other, rows, d_middle, gain, cot, late):
    tile = pl.BlockSpec((BLOCK, 1024), lambda i: (i, 0))
    span = pl.BlockSpec((SPAN, 1024), lambda i: (i, 0))
    return kernel_call(
        input_back_kernel,
        "input_back",
        [struct(cot.shape, BF), struct((8, 1024), F32)],
        us=4,
        late=late,
        grid=(2,),
        in_specs=[
            SMEM,
            SMEM,
            tile,
            tile,
            tile,
            tile,
            pl.BlockSpec((1, 1024), lambda i: (0, 0)),
            span,
        ],
        out_specs=[span, pl.BlockSpec((8, 1024), lambda i: (0, 0))],
    )(groups, shares, part, other, rows, d_middle, gain, cot)


def body(
    tokens,
    norm1_gain,
    norm1_bias,
    qkv_weight,
    query_bias,
    value_bias,
    out_weight,
    out_bias,
    norm2_gain,
    norm2_bias,
    fc1_weight,
    fc1_bias,
    fc2_weight,
    fc2_bias,
    cotangent,
    group_of,
    keep_mask,
    group_tokens,
):
    here = Where()
    own_rows, width = tokens.shape
    c = here.c
    here.make_table()
    place_table = here.table

    vectors = (
        norm1_gain,
        norm1_bias,
        query_bias,
        value_bias,
        out_bias,
        norm2_gain,
        norm2_bias,
        fc2_bias,
        fc1_bias,
    )

    def whole(v):
        return pl.BlockSpec(v.shape, lambda i: (0,) * len(v.shape))

    shapes = [
        struct(shape, BF) for shape in ((8, 32, 1664), (64, 2048), (256, 1024), (64, 1024))
    ]
    weights = (qkv_weight, fc1_weight, fc2_weight, out_weight)
    qkv_rep, fc1_part, fc2_half, out_half = kernel_call(
        prepare_kernel,
        "prepare",
        shapes,
        us=3,
        pinned=range(1, 14),
        grid=(1,),
        in_specs=[SMEM] + [whole(v) for v in weights + vectors],
        out_specs=[whole(v) for v in shapes],
    )(place_table, *weights, *vectors)
    qkv_slab = all_to_all(qkv_rep, "fsdp")
    fc1_row = lax.all_gather(fc1_part, "fsdp", axis=0, axis_index_groups=X_GROUPS)
    out_all = lax.all_gather(out_half, "fsdp", axis=0, tiled=True)
    fc2_pair = assemble(
        here,
        "fc2_hi",
        [fc2_half, permute(fc2_half, flip_hi)],
        (2, 256, 1024),
        lambda o, t, n: o.at[t[HI] if n == 0 else 1 - t[HI]],
    )

    qkv_blocks = ring_blocks(qkv_slab, "z")
    fc1_blocks = ring_blocks(fc1_row, "y")
    fc2_blocks = ring_blocks(fc2_pair, "x")
    qkv_all = assemble(
        here,
        "qkv_z",
        qkv_blocks,
        (8, 4, 32, 1536),
        lambda o, t, n: o.at[:, source_in(t, Z, n)],
        lambda ref: ref.at[:, :, pl.ds(0, 1536)],
        late=fc2_blocks[3:],
    ).reshape(1024, 1536)
    (
        gain_one,
        shift_one,
        out_shift,
        gain_two,
        shift_two,
        fc2_shift,
        query_shift,
        value_shift,
        fc1_shift,
    ) = kernel_call(
        vectors_kernel,
        "vectors",
        [struct((1, 1024), F32)] * 6 + [struct((1, 512), F32)] * 2 + [struct((1, 2048), F32)],
        us=1,
        grid=(1,),
        in_specs=[SMEM, pl.BlockSpec((8, 16, 128), lambda i: (0, 0, 12))],
        out_specs=[pl.BlockSpec((1, n), lambda i: (0, 0)) for n in (1024,) * 6 + (512,) * 2 + (2048,)],
    )(place_table, qkv_slab)

    groups = jnp.stack([pick(group_of, here.dp), pick(group_of, here.dp + here.sign)])
    counts = group_tokens.astype(F32)
    shares = counts / jnp.sum(counts)
    shares = jnp.where(groups == 1, shares[1], shares[0])
    rows_low, cot, d_branch, mask_col, blocked = compact(
        groups,
        shares,
        tokens,
        permute(tokens, swap_core),
        cotangent,
        permute(cotangent, swap_core),
        keep_mask,
        permute(keep_mask, swap_core),
    )
    own_rows = 2 * BLOCK

    yhat_one, _ = normalize(rows_low.astype(F32))
    normed = (yhat_one * gain_one + shift_one).astype(BF)
    packed = dot(normed, qkv_all)
    mixed, attention_done = attention(packed, query_shift, value_shift, blocked, fc1_blocks[3:])
    attended = dot(mixed, out_all).astype(BF)
    middle, normed_two = middle_layer(
        attended, permute(attended, swap_core), rows_low, mask_col, out_shift, gain_two, shift_two
    )
    fc1_all = assemble(
        here,
        "fc1_y",
        fc1_blocks,
        (2, 4, 2, 64, 2048),
        lambda o, t, n: o.at[source_in(t, Y, n) // 2, :, lax.rem(source_in(t, Y, n), 2)],
        late=(attention_done,),
    ).reshape(1024, 2048)
    hidden, slope = hidden_layer(normed_two, fc1_all, fc1_shift)
    fc2_all = assemble(
        here,
        "fc2_x",
        fc2_blocks,
        (2, 4, 256, 1024),
        lambda o, t, n: o.at[:, source_in(t, X, n)],
        late=(attention_done,),
    ).reshape(2048, 1024)

    grad_fc2, fc2_done = grad_fc2_terms(hidden, d_branch, ())
    fc2_sum = lax.psum_scatter(
        grad_fc2.reshape(2048, 1024),
        "dp",
        scatter_dimension=0,
        axis_index_groups=Z_GROUPS,
        tiled=True,
    )
    d_pre, fc1_bias_sum = hidden_back(d_branch, fc2_all, slope, (fc2_done,))
    d_normed_two = dot_nt(d_pre, fc1_all).astype(BF)
    *grad_fc1, fc1_done = grad_fc1_terms(here, normed_two, d_pre, (d_normed_two,))
    fc1_arrived = permute(grad_fc1[0], ring_move("y"))
    d_middle, d_attended, middle_sums = middle_back(
        shares,
        d_normed_two,
        permute(d_normed_two, swap_core),
        middle,
        cot,
        mask_col,
        gain_two,
        (fc1_done,),
    )
    d_mixed = dot_nt(d_attended, out_all).astype(BF)
    d_packed, packed_sums = attention_back(
        packed, query_shift, value_shift, blocked, d_mixed, ()
    )
    fc1_sum, add_done = sum_of("fc1_add", (fc1_arrived, grad_fc1[1]), (packed_sums,))
    fc1_arrived = permute(fc1_sum, ring_move("y"))
    grad_qkv = grad_qkv_terms(normed, d_packed, mixed, d_attended, (add_done,))
    grad_qkv, d_packed, hidden = lax.optimization_barrier((grad_qkv, d_packed, hidden))
    qkv_sum = lax.psum_scatter(
        grad_qkv.reshape(1024, 2048),
        "dp",
        scatter_dimension=0,
        axis_index_groups=Z_GROUPS,
        tiled=True,
    ).reshape(8, 32, 2048)
    fc2_sum = all_to_all(fc2_sum.reshape(8, 64, 1024), "fsdp")
    fc2_kept, fc2_sent, _ = sum_and_halve(here, "fc2_lo", fc2_sum, 1024)
    fc1_sum, _ = sum_of("fc1_add", (fc1_arrived, grad_fc1[2]), (fc2_kept,))
    fc1_arrived = permute(fc1_sum, ring_move("y"))
    fc1_sum, _ = sum_of("fc1_add", (fc1_arrived, grad_fc1[3]))
    fc1_sum = all_to_all(fc1_sum, "fsdp", X_GROUPS)
    fc1_sum = sum_first("fc1_sum", fc1_sum).reshape(4, 16, 2048)
    fc1_sum = all_to_all(fc1_sum, "dp", Z_GROUPS)

    d_normed_sent = permute(dot_nt(d_packed[own_rows:], qkv_all).astype(BF), swap_core)
    d_normed_own = dot_nt(d_packed[:own_rows], qkv_all).astype(BF)
    input_grad, input_sums = input_back(
        groups,
        shares,
        d_normed_own,
        d_normed_sent,
        rows_low,
        d_middle,
        gain_one,
        cotangent,
        (),
    )

    branch_sent = permute(dot(hidden[own_rows:], fc2_all).astype(BF), swap_core)
    block_out, block_done = block_out_layer(
        groups,
        dot(hidden[:own_rows], fc2_all),
        branch_sent,
        middle,
        mask_col,
        fc2_shift,
        tokens,
    )

    vector_terms = kernel_call(
        vector_terms_kernel,
        "vector_terms",
        struct((8, 16, 128), F32),
        us=1,
        in_specs=[SMEM] + [VMEM] * 4,
        out_specs=VMEM,
    )(place_table, input_sums, packed_sums, middle_sums, fc1_bias_sum)
    qkv_sum = join(qkv_sum, vector_terms, (block_done, fc2_kept, fc1_sum))
    qkv_sum = all_to_all(qkv_sum, "fsdp")
    qkv_kept, qkv_sent, vector_sums = sum_and_halve(here, "qkv_lo", qkv_sum, 2048)
    sums = (qkv_kept, qkv_sent, fc2_kept, fc2_sent, fc1_sum, vector_sums)
    packed_slices = kernel_call(
        pack_kernel,
        "pack",
        struct((8, 48, 2176), BF),
        us=1.5,
        grid=(1,),
        in_specs=[whole(v) for v in sums],
        out_specs=whole(struct((8, 48, 2176), BF)),
    )(*sums)
    own = all_to_all(packed_slices, "dp", SLICE_GROUPS)
    half = pl.BlockSpec((None, 48, 2176), lambda i: (i, 0, 0))
    grad_qkv_weight, grad_out_weight, grad_fc1_weight, grad_fc2_weight, *vector_sums = kernel_call(
        unpack_kernel,
        "unpack",
        [
            struct((128, 3072), F32),
            struct((2, 8, 8, 1024), F32),
            struct((128, 4096), F32),
            struct((2, 8, 32, 1024), F32),
            *(struct((1, 128), F32),) * 8,
            struct((4, 128), F32),
        ],
        us=5,
        grid=(8,),
        in_specs=[SMEM, half, half],
        out_specs=[
            pl.BlockSpec((16, 3072), lambda i: (i, 0)),
            pl.BlockSpec((2, None, 8, 1024), lambda i: (0, i, 0, 0)),
            pl.BlockSpec((16, 4096), lambda i: (lax.rem(i, 2) * 4 + i // 2, 0)),
            pl.BlockSpec((2, None, 32, 1024), lambda i: (0, i, 0, 0)),
            *(pl.BlockSpec((1, 128), lambda i: (0, 0)),) * 8,
            pl.BlockSpec((4, 128), lambda i: (0, 0)),
        ],
    )(place_table, own, permute(own, swap_core))
    return (
        block_out,
        input_grad,
        vector_sums[0].reshape(128),
        vector_sums[1].reshape(128),
        grad_qkv_weight,
        vector_sums[2].reshape(128),
        vector_sums[3].reshape(128),
        grad_out_weight.reshape(128, 1024),
        vector_sums[4].reshape(128),
        vector_sums[5].reshape(128),
        vector_sums[6].reshape(128),
        grad_fc1_weight,
        vector_sums[8].reshape(512),
        grad_fc2_weight.reshape(512, 1024),
        vector_sums[7].reshape(128),
    )


def solution(mesh):
    rows, cols, both = P("fsdp", None), P("fsdp"), ("dp", "fsdp")
    in_specs = (
        P(both, None),
        cols,
        cols,
        rows,
        cols,
        cols,
        rows,
        cols,
        cols,
        cols,
        rows,
        cols,
        rows,
        cols,
        P(both, None),
        P(),
        P(both),
        P(),
    )
    out_specs = (
        P(both, None),
        P(both, None),
        cols,
        cols,
        rows,
        cols,
        cols,
        rows,
        cols,
        cols,
        cols,
        rows,
        cols,
        rows,
        cols,
    )
    return jax.shard_map(body, mesh=mesh, in_specs=in_specs, out_specs=out_specs, check_vma=False)
```

profile of v0, /device:TPU:1, one launch (start us, length us, event | category | flops | bytes accessed | tf_op | source)
XLA Modules:
  0.0 327.7 jit_solution(15201096982828198854)
XLA Ops:
  11.4 3.6 %collective-permute-start.6 = (bf16[256,1024]{1,0:T(8,128)(2,1)S(1)}, bf16[256,1024]{1,0:T(8,128)(2,1)}, u32[]{:S(2)}, u32[]{:S(2)}) collective-permute-start(bf16[256,1024]{1,0:T(8,128)(2,1)S(1)} %get-tuple-element.86.refs_1_), channel_id=1, source_target_pairs={{0,68},{1,69},{2,70},{3,71},{4,64},{5,65},{6,66},{7,67},{8,76},{9,... | collective-permute-start | bytes 1572872 | tf_op jit(solution)/shard_map/ppermute | solution.py:38
  15.0 4.2 %all-to-all-start = ((bf16[8,32,1664]{2,1,0:T(8,128)(2,1)}), bf16[8,32,1664]{2,1,0:T(8,128)(2,1)S(1)}, u32[]{:S(2)}, u32[]{:S(2)}) async-start(bf16[8,32,1664]{2,1,0:T(8,128)(2,1)} %get-tuple-element.83), calls=%async_computation | async-start | bytes 1703936 | tf_op jit(solution)/shard_map/all_to_all | solution.py:649
  19.3 15.2 %collective-permute-done.6.refs_2_ = bf16[256,1024]{1,0:T(8,128)(2,1)} collective-permute-done((bf16[256,1024]{1,0:T(8,128)(2,1)S(1)}, bf16[256,1024]{1,0:T(8,128)(2,1)}, u32[]{:S(2)}, u32[]{:S(2)}) %collective-permute-start.6) | collective-permute-done | bytes 524320 | tf_op jit(solution)/shard_map/ppermute | solution.py:38
  36.2 3.7 %collective-permute-start.7 = (bf16[2,256,1024]{2,1,0:T(8,128)(2,1)S(1)}, bf16[2,256,1024]{2,1,0:T(8,128)(2,1)}, u32[]{:S(2)}, u32[]{:S(2)}) collective-permute-start(bf16[2,256,1024]{2,1,0:T(8,128)(2,1)S(1)} %fc2_hi.1.refs_1_), channel_id=1, source_target_pairs={{0,1},{1,2},{2,3},{3,0},{4,5},{5,6},{6,7},{7,4},{8,11},{9,8},{10,9... | collective-permute-start | bytes 3145736 | tf_op jit(solution)/shard_map/ppermute | solution.py:38
  43.1 4.1 %collective-permute-start.3 = (bf16[8,32,1664]{2,1,0:T(8,128)(2,1)S(1)}, bf16[8,32,1664]{2,1,0:T(8,128)(2,1)}, u32[]{:S(2)}, u32[]{:S(2)}) collective-permute-start(bf16[8,32,1664]{2,1,0:T(8,128)(2,1)S(1)} %all-to-all-done.refs_1_), channel_id=1, source_target_pairs={{0,16},{1,17},{2,18},{3,19},{4,20},{5,21},{6,22},{7,23},{8,56},{9,... | collective-permute-start | bytes 2555912 | tf_op jit(solution)/shard_map/ppermute | solution.py:38
  47.2 4.5 %collective-permute-done.7.refs_2_ = bf16[2,256,1024]{2,1,0:T(8,128)(2,1)} collective-permute-done((bf16[2,256,1024]{2,1,0:T(8,128)(2,1)S(1)}, bf16[2,256,1024]{2,1,0:T(8,128)(2,1)}, u32[]{:S(2)}, u32[]{:S(2)}) %collective-permute-start.7) | collective-permute-done | bytes 1048608 | tf_op jit(solution)/shard_map/ppermute | solution.py:38
  51.7 3.5 %collective-permute-start.8 = (bf16[2,256,1024]{2,1,0:T(8,128)(2,1)}, bf16[2,256,1024]{2,1,0:T(8,128)(2,1)}, u32[]{:S(2)}, u32[]{:S(2)}) collective-permute-start(bf16[2,256,1024]{2,1,0:T(8,128)(2,1)} %collective-permute-done.7.refs_2_), channel_id=1, source_target_pairs={{0,1},{1,2},{2,3},{3,0},{4,5},{5,6},{6,7},{7,4},{8,11},{9,8},{10,9... | collective-permute-start | bytes 3145736 | tf_op jit(solution)/shard_map/ppermute | solution.py:38
  56.8 3.5 %collective-permute-start.4 = (bf16[8,32,1664]{2,1,0:T(8,128)(2,1)}, bf16[8,32,1664]{2,1,0:T(8,128)(2,1)}, u32[]{:S(2)}, u32[]{:S(2)}) collective-permute-start(bf16[8,32,1664]{2,1,0:T(8,128)(2,1)} %collective-permute-done.3.refs_2_), channel_id=1, source_target_pairs={{0,16},{1,17},{2,18},{3,19},{4,20},{5,21},{6,22},{7,23},{8,56},{9,... | collective-permute-start | bytes 2555912 | tf_op jit(solution)/shard_map/ppermute | solution.py:38
  69.9 3.4 %compact.1 = (bf16[640,1024]{1,0:T(8,128)(2,1)S(1)}, bf16[640,1024]{1,0:T(8,128)(2,1)S(1)}, bf16[640,1024]{1,0:T(8,128)(2,1)S(1)}, f32[640,1]{1,0:T(8,128)S(1)}, f32[4,160,160]{2,1,0:T(8,128)S(1)}) custom-call(s32[2]{0:T(128)S(1)} %get-tuple-element.150.refs_0_, f32[2]{0:T(128)S(1)} %get-tuple-element.149.refs_1_.refs_0_, bf16[384,1024]{1,0:T(8,128)(2,1)S(1)} %copy-done.26, ...), custom_call_target="tpu_custom_call" | custom-call | flops 1437500032 | bytes 65536 | tf_op jit(solution)/shard_map/compact/pallas_call | solution.py:186
  80.8 9.0 %collective-permute-done.5.refs_4_ = bf16[8,32,1664]{2,1,0:T(8,128)(2,1)S(1)} collective-permute-done((bf16[8,32,1664]{2,1,0:T(8,128)(2,1)}, bf16[8,32,1664]{2,1,0:T(8,128)(2,1)S(1)}, u32[]{:S(2)}, u32[]{:S(2)}) %collective-permute-start.5) | collective-permute-done | bytes 852000 | tf_op jit(solution)/shard_map/ppermute | solution.py:38
  98.9 5.0 %attention.1 = (bf16[640,512]{1,0:T(8,128)(2,1)S(1)}, f32[8,128]{1,0:T(8,128)S(1)}) custom-call(f32[640,1536]{1,0:T(8,128)S(1)} %fusion.13.refs_0_, f32[1,512]{1,0:T(1,128)S(1)} %get-tuple-element.87.refs_1_, f32[1,512]{1,0:T(1,128)S(1)} %get-tuple-element.88.refs_2_, f32[4,160,160]{2,1,0:T(8,128)S(1)} %get-tuple-element.89.refs_3_, ...), custom_call_target="tpu_custom_call" | custom-call | flops 1437500032 | bytes 65536 | tf_op jit(solution)/shard_map/attention/pallas_call | solution.py:186
  112.1 3.2 middle_layer.1
  115.3 8.7 %hidden_layer.1 = (bf16[640,2048]{1,0:T(8,128)(2,1)S(1)}, bf16[640,2048]{1,0:T(8,128)(2,1)S(1)}) custom-call(bf16[640,1024]{1,0:T(8,128)(2,1)S(1)} %get-tuple-element.99.refs_0_.refs_1_, bf16[1024,2048]{1,0:T(8,128)(2,1)S(1)} %bitcast.45, f32[1,2048]{1,0:T(1,128)S(1)} %get-tuple-element.100.refs_2_), custom_call_target="tpu_custom_call" | custom-call | flops 3162500096 | bytes 65536 | tf_op jit(solution)/shard_map/hidden_layer/pallas_call | solution.py:186
  124.1 5.7 %grad_fc2.1 = (bf16[4,8,64,1024]{3,2,1,0:T(8,128)(2,1)}, f32[8,128]{1,0:T(8,128)S(1)}) custom-call(bf16[640,2048]{1,0:T(8,128)(2,1)S(1)} %get-tuple-element.114.refs_0_, bf16[640,1024]{1,0:T(8,128)(2,1)S(1)} %copy-done.20), custom_call_target="tpu_custom_call" | custom-call | flops 1437500032 | bytes 65536 | tf_op jit(solution)/shard_map/grad_fc2/pallas_call | solution.py:186
  133.3 5.1 %hidden_back.1 = (bf16[640,2048]{1,0:T(8,128)(2,1)S(1)}, f32[1,2048]{1,0:T(1,128)S(1)}) custom-call(bf16[640,1024]{1,0:T(8,128)(2,1)S(1)} %copy-done.21, bf16[2048,1024]{1,0:T(8,128)(2,1)S(1)} %bitcast.42, bf16[640,2048]{1,0:T(8,128)(2,1)S(1)} %copy-done.11, f32[8,128]{1,0:T(8,128)S(1)} %get-tuple-element.103.refs_3_), custom_call_target="tpu_custom_call" | custom-call | flops 1724999936 | bytes 65536 | tf_op jit(solution)/shard_map/hidden_back/pallas_call | solution.py:186
  142.4 6.9 %grad_fc1.1 = (bf16[4,64,2048]{2,1,0:T(8,128)(2,1)}, bf16[4,64,2048]{2,1,0:T(8,128)(2,1)}, bf16[4,64,2048]{2,1,0:T(8,128)(2,1)}, bf16[4,64,2048]{2,1,0:T(8,128)(2,1)}, f32[8,128]{1,0:T(8,128)S(1)}) custom-call(s32[6]{0:T(128)S(1)} %stack.33.refs_0_, bf16[640,1024]{1,0:T(8,128)(2,1)S(1)} %copy-done.50, bf16[640,2048]{1,0:T(8,128)(2,1)S(1)} %get-tuple-element.104.refs_2_, ...), custom_call_target="tpu_custom_call" | custom-call | flops 1437500032 | bytes 65536 | tf_op jit(solution)/shard_map/grad_fc1/pallas_call | solution.py:186
  152.5 5.0 %middle_back.1 = (f32[640,1024]{1,0:T(8,128)S(1)}, bf16[640,1024]{1,0:T(8,128)(2,1)S(1)}, f32[8,1024]{1,0:T(8,128)S(1)}) custom-call(f32[2]{0:T(128)S(1)} %get-tuple-element.149.refs_1_.refs_0_, bf16[640,1024]{1,0:T(8,128)(2,1)S(1)} %copy-done.40, bf16[640,1024]{1,0:T(8,128)(2,1)S(1)} %collective-permute-done.14.refs_2_, ...), custom_call_target="tpu_custom_call" | custom-call | flops 2012499968 | bytes 65536 | tf_op jit(solution)/shard_map/middle_back/pallas_call | solution.py:186
  161.7 10.4 %attention_back.1 = (bf16[640,1536]{1,0:T(8,128)(2,1)S(1)}, f32[1,1536]{1,0:T(1,128)S(1)}) custom-call(f32[640,1536]{1,0:T(8,128)S(1)} %copy-done.6, f32[1,512]{1,0:T(1,128)S(1)} %get-tuple-element.87.refs_1_, f32[1,512]{1,0:T(1,128)S(1)} %get-tuple-element.88.refs_2_, f32[4,160,160]{2,1,0:T(8,128)S(1)} %copy-done.31, ...), custom_call_target="tpu_custom_call" | custom-call | flops 4600000000 | bytes 65536 | tf_op jit(solution)/shard_map/attention_back/pallas_call | solution.py:186
  172.5 5.4 %grad_qkv.1 = bf16[4,8,32,2048]{3,2,1,0:T(8,128)(2,1)} custom-call(bf16[640,1024]{1,0:T(8,128)(2,1)S(1)} %fusion.5.refs_0_, bf16[640,1536]{1,0:T(8,128)(2,1)S(1)} %get-tuple-element.117.refs_1_, bf16[640,512]{1,0:T(8,128)(2,1)S(1)} %get-tuple-element.93.refs_2_, bf16[640,1024]{1,0:T(8,128)(2,1)S(1)} %get-tuple-element.108.refs_3_, ...), custom_call_target="tpu_custom_call" | custom-call | flops 1437500032 | bytes 65536 | tf_op jit(solution)/shard_map/grad_qkv/pallas_call | solution.py:186
  178.1 21.0 %all_to_all.30.refs_1_ = bf16[8,64,1024]{2,1,0:T(8,128)(2,1)S(1)} all-to-all(bf16[8,64,1024]{2,1,0:T(8,128)(2,1)} %bitcast.55), channel_id=1, replica_groups=mesh['dp'=16,'fsdp'=8] {'fsdp'}, dimensions={0} | all-to-all | bytes 2097152 | tf_op jit(solution)/shard_map/all_to_all | solution.py:649
  202.8 5.2 %collective-permute-start.19 = (bf16[4,64,2048]{2,1,0:T(8,128)(2,1)S(1)}, bf16[4,64,2048]{2,1,0:T(8,128)(2,1)S(1)}, u32[]{:S(2)}, u32[]{:S(2)}) collective-permute-start(bf16[4,64,2048]{2,1,0:T(8,128)(2,1)S(1)} %get-tuple-element.129), channel_id=1, source_target_pairs={{0,64},{1,65},{2,66},{3,67},{4,68},{5,69},{6,70},{7,71},{8,76},{9,... | collective-permute-start | bytes 3145736 | tf_op jit(solution)/shard_map/ppermute | solution.py:38
  213.3 6.4 %collective-permute-done.19.refs_0_ = bf16[4,64,2048]{2,1,0:T(8,128)(2,1)S(1)} collective-permute-done((bf16[4,64,2048]{2,1,0:T(8,128)(2,1)S(1)}, bf16[4,64,2048]{2,1,0:T(8,128)(2,1)S(1)}, u32[]{:S(2)}, u32[]{:S(2)}) %collective-permute-start.19) | collective-permute-done | bytes 1048608 | tf_op jit(solution)/shard_map/ppermute | solution.py:38
  220.8 4.2 %all-to-all-start.2 = ((bf16[4,64,2048]{2,1,0:T(8,128)(2,1)}), bf16[4,64,2048]{2,1,0:T(8,128)(2,1)S(1)}, u32[]{:S(2)}, u32[]{:S(2)}) async-start(bf16[4,64,2048]{2,1,0:T(8,128)(2,1)} %get-tuple-element.131), calls=%async_computation.4 | async-start | bytes 2097152 | tf_op jit(solution)/shard_map/all_to_all | solution.py:649
  225.0 4.4 %convolution_convert_fusion.3.refs_2_ = bf16[320,1024]{1,0:T(8,128)(2,1)} fusion(bf16[1024,1536]{1,0:T(8,128)(2,1)} %bitcast.48, bf16[640,1536]{1,0:T(8,128)(2,1)} %copy-done.17), kind=kOutput, calls=%fused_computation.11 | convolution fusion | flops 1006960640 | bytes 4784128 | tf_op jit(solution)/shard_map/dot_general | solution.py:847
  232.1 4.0 %all-to-all-done.2.refs_0_ = bf16[4,64,2048]{2,1,0:T(8,128)(2,1)S(1)} async-done(((bf16[4,64,2048]{2,1,0:T(8,128)(2,1)}), bf16[4,64,2048]{2,1,0:T(8,128)(2,1)S(1)}, u32[]{:S(2)}, u32[]{:S(2)}) %all-to-all-start.2) | async-done | bytes 1048608 | tf_op jit(solution)/shard_map/all_to_all | solution.py:649
  236.9 3.7 %all-to-all-start.3 = ((bf16[4,16,2048]{2,1,0:T(8,128)(2,1)}), bf16[4,16,2048]{2,1,0:T(8,128)(2,1)S(1)}, u32[]{:S(2)}, u32[]{:S(2)}) async-start(bf16[4,16,2048]{2,1,0:T(8,128)(2,1)} %bitcast.18), calls=%async_computation.5 | async-start | bytes 524288 | tf_op jit(solution)/shard_map/all_to_all | solution.py:649
  243.5 3.6 %input_back.1 = (bf16[384,1024]{1,0:T(8,128)(2,1)}, f32[8,1024]{1,0:T(8,128)S(1)}) custom-call(s32[2]{0:T(128)S(1)} %get-tuple-element.150.refs_0_, f32[2]{0:T(128)S(1)} %copy-done.38, bf16[320,1024]{1,0:T(8,128)(2,1)S(1)} %copy-done.32, bf16[320,1024]{1,0:T(8,128)(2,1)} %collective-permute-done.17.refs_3_, ...), custom_call_target="tpu_custom_call" | custom-call | flops 1150000000 | bytes 65536 | tf_op jit(solution)/shard_map/input_back/pallas_call | solution.py:186
  253.3 7.8 %all-to-all-start.4 = ((bf16[8,32,2176]{2,1,0:T(8,128)(2,1)}), bf16[8,32,2176]{2,1,0:T(8,128)(2,1)S(1)}, u32[]{:S(2)}, u32[]{:S(2)}) async-start(bf16[8,32,2176]{2,1,0:T(8,128)(2,1)} %join.1), calls=%async_computation.6 | async-start | bytes 2228224 | tf_op jit(solution)/shard_map/all_to_all | solution.py:649
  264.0 15.1 %all-to-all-done.4.refs_1_ = bf16[8,32,2176]{2,1,0:T(8,128)(2,1)S(1)} async-done(((bf16[8,32,2176]{2,1,0:T(8,128)(2,1)}), bf16[8,32,2176]{2,1,0:T(8,128)(2,1)S(1)}, u32[]{:S(2)}, u32[]{:S(2)}) %all-to-all-start.4) | async-done | bytes 1114144 | tf_op jit(solution)/shard_map/all_to_all | solution.py:649
  284.5 25.2 %all_to_all.31.refs_1_ = bf16[8,48,2176]{2,1,0:T(8,128)(2,1)S(1)} all-to-all(bf16[8,48,2176]{2,1,0:T(8,128)(2,1)S(1)} %pack.1), channel_id=1, replica_groups={{0,64,16,80,32,96,48,112},{8,72,24,88,40,104,56,120},{1,65,17,81,33,97,..., dimensions={0} | all-to-all | bytes 3342336 | tf_op jit(solution)/shard_map/all_to_all | solution.py:649
  309.7 3.2 collective-permute-start.22
  316.1 4.5 %unpack.1 = (f32[128,3072]{1,0:T(8,128)}, f32[2,8,8,1024]{3,2,1,0:T(8,128)}, f32[128,4096]{1,0:T(8,128)}, f32[2,8,32,1024]{3,2,1,0:T(8,128)}, f32[1,128]{1,0:T(1...) custom-call(s32[6]{0:T(128)S(1)} %stack.33.refs_0_, ...), custom_call_target="tpu_custom_call" | custom-call | flops 1437500032 | bytes 65536 | tf_op jit(solution)/shard_map/unpack/pallas_call | solution.py:186
  (217 shorter events, 93.3 us)
Async XLA Ops:
  8.0 32.9 %all-gather.6.cloned.1.call-start = ((), (), s32[]{:S(2)}) async-start(), calls=%async_computation.11 | async-start | bytes 1310720 | tf_op jit(solution)/shard_map/all_gather | solution.py:1037
  11.4 23.1 %collective-permute-start.6 = (bf16[256,1024]{1,0:T(8,128)(2,1)S(1)}, bf16[256,1024]{1,0:T(8,128)(2,1)}, u32[]{:S(2)}, u32[]{:S(2)}) collective-permute-start(bf16[256,1024]{1,0:T(8,128)(2,1)S(1)} %get-tuple-element.86.refs_1_), channel_id=1, source_target_pairs={{0,68},{1,69},{2,70},{3,71},{4,64},{5,65},{6,66},{7,67},{8,76},{9,... | collective-permute-start | bytes 1572872 | tf_op jit(solution)/shard_map/ppermute | solution.py:38
  15.0 28.1 %all-to-all-start = ((bf16[8,32,1664]{2,1,0:T(8,128)(2,1)}), bf16[8,32,1664]{2,1,0:T(8,128)(2,1)S(1)}, u32[]{:S(2)}, u32[]{:S(2)}) async-start(bf16[8,32,1664]{2,1,0:T(8,128)(2,1)} %get-tuple-element.83), calls=%async_computation | async-start | bytes 1703936 | tf_op jit(solution)/shard_map/all_to_all | solution.py:649
  19.2 86.5 %all-gather.4.cloned.1.call-start = ((), (), s32[]{:S(2)}) async-start(), calls=%async_computation.8 | async-start | bytes 1179648 | tf_op jit(solution)/shard_map/all_gather | solution.py:1038
  36.2 15.5 %collective-permute-start.7 = (bf16[2,256,1024]{2,1,0:T(8,128)(2,1)S(1)}, bf16[2,256,1024]{2,1,0:T(8,128)(2,1)}, u32[]{:S(2)}, u32[]{:S(2)}) collective-permute-start(bf16[2,256,1024]{2,1,0:T(8,128)(2,1)S(1)} %fc2_hi.1.refs_1_), channel_id=1, source_target_pairs={{0,1},{1,2},{2,3},{3,0},{4,5},{5,6},{6,7},{7,4},{8,11},{9,8},{10,9... | collective-permute-start | bytes 3145736 | tf_op jit(solution)/shard_map/ppermute | solution.py:38
  40.9 20.1 %collective-permute-start.10 = (bf16[4,64,2048]{2,1,0:T(8,128)(2,1)}, bf16[4,64,2048]{2,1,0:T(8,128)(2,1)}, u32[]{:S(2)}, u32[]{:S(2)}) collective-permute-start(bf16[4,64,2048]{2,1,0:T(8,128)(2,1)} %bitcast.56), channel_id=1, source_target_pairs={{0,64},{1,65},{2,66},{3,67},{4,68},{5,69},{6,70},{7,71},{8,76},{9,... | collective-permute-start | bytes 3145736 | tf_op jit(solution)/shard_map/ppermute | solution.py:38
  43.1 13.8 %collective-permute-start.3 = (bf16[8,32,1664]{2,1,0:T(8,128)(2,1)S(1)}, bf16[8,32,1664]{2,1,0:T(8,128)(2,1)}, u32[]{:S(2)}, u32[]{:S(2)}) collective-permute-start(bf16[8,32,1664]{2,1,0:T(8,128)(2,1)S(1)} %all-to-all-done.refs_1_), channel_id=1, source_target_pairs={{0,16},{1,17},{2,18},{3,19},{4,20},{5,21},{6,22},{7,23},{8,56},{9,... | collective-permute-start | bytes 2555912 | tf_op jit(solution)/shard_map/ppermute | solution.py:38
  51.7 22.7 %collective-permute-start.8 = (bf16[2,256,1024]{2,1,0:T(8,128)(2,1)}, bf16[2,256,1024]{2,1,0:T(8,128)(2,1)}, u32[]{:S(2)}, u32[]{:S(2)}) collective-permute-start(bf16[2,256,1024]{2,1,0:T(8,128)(2,1)} %collective-permute-done.7.refs_2_), channel_id=1, source_target_pairs={{0,1},{1,2},{2,3},{3,0},{4,5},{5,6},{6,7},{7,4},{8,11},{9,8},{10,9... | collective-permute-start | bytes 3145736 | tf_op jit(solution)/shard_map/ppermute | solution.py:38
  55.2 1.2 collective-permute-start.2
  55.2 13.5 %collective-permute-start = (bf16[384,1024]{1,0:T(8,128)(2,1)S(1)}, bf16[384,1024]{1,0:T(8,128)(2,1)}, u32[]{:S(2)}, u32[]{:S(2)}) collective-permute-start(bf16[384,1024]{1,0:T(8,128)(2,1)S(1)} %copy-done.26), channel_id=1, source_target_pairs={{0,8},{1,9},{2,10},{3,11},{4,12},{5,13},{6,14},{7,15},{8,0},{9,1},... | collective-permute-start | bytes 2359304 | tf_op jit(solution)/shard_map/ppermute | solution.py:38
  56.4 12.4 %collective-permute-start.1 = (bf16[384,1024]{1,0:T(8,128)(2,1)}, bf16[384,1024]{1,0:T(8,128)(2,1)}, u32[]{:S(2)}, u32[]{:S(2)}) collective-permute-start(bf16[384,1024]{1,0:T(8,128)(2,1)} %refs_7_.3), channel_id=1, source_target_pairs={{0,8},{1,9},{2,10},{3,11},{4,12},{5,13},{6,14},{7,15},{8,0},{9,1},... | collective-permute-start | bytes 2359304 | tf_op jit(solution)/shard_map/ppermute | solution.py:38
  56.6 121.5 %reduce-scatter.5.cloned.1.call-start = ((), (), s32[]{:S(2)}) async-start(), calls=%async_computation.10 | async-start | bytes 5242880 | tf_op jit(solution)/shard_map/reduce_scatter | solution.py:1122
  56.8 20.8 %collective-permute-start.4 = (bf16[8,32,1664]{2,1,0:T(8,128)(2,1)}, bf16[8,32,1664]{2,1,0:T(8,128)(2,1)}, u32[]{:S(2)}, u32[]{:S(2)}) collective-permute-start(bf16[8,32,1664]{2,1,0:T(8,128)(2,1)} %collective-permute-done.3.refs_2_), channel_id=1, source_target_pairs={{0,16},{1,17},{2,18},{3,19},{4,20},{5,21},{6,22},{7,23},{8,56},{9,... | collective-permute-start | bytes 2555912 | tf_op jit(solution)/shard_map/ppermute | solution.py:38
  61.0 17.4 %collective-permute-start.11 = (bf16[4,64,2048]{2,1,0:T(8,128)(2,1)}, bf16[4,64,2048]{2,1,0:T(8,128)(2,1)}, u32[]{:S(2)}, u32[]{:S(2)}) collective-permute-start(bf16[4,64,2048]{2,1,0:T(8,128)(2,1)} %collective-permute-done.10.refs_2_), channel_id=1, source_target_pairs={{0,64},{1,65},{2,66},{3,67},{4,68},{5,69},{6,70},{7,71},{8,76},{9,... | collective-permute-start | bytes 3145736 | tf_op jit(solution)/shard_map/ppermute | solution.py:38
  68.0 83.2 %copy-start.37 = (f32[2]{0:T(128)}, f32[2]{0:T(128)S(1)}, u32[]{:S(2)}) copy-start(f32[2]{0:T(128)S(1)} %get-tuple-element.149.refs_1_.refs_0_) | copy-start | bytes 28
  74.4 16.9 %collective-permute-start.9 = (bf16[2,256,1024]{2,1,0:T(8,128)(2,1)}, bf16[2,256,1024]{2,1,0:T(8,128)(2,1)S(1)}, u32[]{:S(2)}, u32[]{:S(2)}) collective-permute-start(bf16[2,256,1024]{2,1,0:T(8,128)(2,1)} %collective-permute-done.8.refs_3_), channel_id=1, source_target_pairs={{0,1},{1,2},{2,3},{3,0},{4,5},{5,6},{6,7},{7,4},{8,11},{9,8},{10,9... | collective-permute-start | bytes 3145736 | tf_op jit(solution)/shard_map/ppermute | solution.py:38
  77.7 12.1 %collective-permute-start.5 = (bf16[8,32,1664]{2,1,0:T(8,128)(2,1)}, bf16[8,32,1664]{2,1,0:T(8,128)(2,1)S(1)}, u32[]{:S(2)}, u32[]{:S(2)}) collective-permute-start(bf16[8,32,1664]{2,1,0:T(8,128)(2,1)} %collective-permute-done.4.refs_3_), channel_id=1, source_target_pairs={{0,16},{1,17},{2,18},{3,19},{4,20},{5,21},{6,22},{7,23},{8,56},{9,... | collective-permute-start | bytes 2555912 | tf_op jit(solution)/shard_map/ppermute | solution.py:38
  78.4 19.6 %collective-permute-start.12 = (bf16[4,64,2048]{2,1,0:T(8,128)(2,1)}, bf16[4,64,2048]{2,1,0:T(8,128)(2,1)S(1)}, u32[]{:S(2)}, u32[]{:S(2)}) collective-permute-start(bf16[4,64,2048]{2,1,0:T(8,128)(2,1)} %collective-permute-done.11.refs_3_), channel_id=1, source_target_pairs={{0,64},{1,65},{2,66},{3,67},{4,68},{5,69},{6,70},{7,71},{8,76},{9,... | collective-permute-start | bytes 3145736 | tf_op jit(solution)/shard_map/ppermute | solution.py:38
  107.8 4.2 %collective-permute-start.13 = (bf16[640,1024]{1,0:T(8,128)(2,1)S(1)}, bf16[640,1024]{1,0:T(8,128)(2,1)S(1)}, u32[]{:S(2)}, u32[]{:S(2)}) collective-permute-start(bf16[640,1024]{1,0:T(8,128)(2,1)S(1)} %convolution_convert_fusion.1.refs_0_), channel_id=1, source_target_pairs={{0,8},{1,9},{2,10},{3,11},{4,12},{5,13},{6,14},{7,15},{8,0},{9,1},... | collective-permute-start | bytes 3932168 | tf_op jit(solution)/shard_map/ppermute | solution.py:38
  129.8 120.4 %reduce-scatter.3.cloned.1.call-start = ((), (), s32[]{:S(2)}) async-start(), calls=%async_computation.9 | async-start | bytes 5242880 | tf_op jit(solution)/shard_map/reduce_scatter | solution.py:1151
  141.4 9.9 %collective-permute-start.14 = (bf16[640,1024]{1,0:T(8,128)(2,1)S(1)}, bf16[640,1024]{1,0:T(8,128)(2,1)S(1)}, u32[]{:S(2)}, u32[]{:S(2)}) collective-permute-start(bf16[640,1024]{1,0:T(8,128)(2,1)S(1)} %convolution_convert_fusion.refs_3_.refs_1_), channel_id=1, source_target_pairs={{0,8},{1,9},{2,10},{3,11},{4,12},{5,13},{6,14},{7,15},{8,0},{9,1},... | collective-permute-start | bytes 3932168 | tf_op jit(solution)/shard_map/ppermute | solution.py:38
  149.2 22.9 %collective-permute-start.15 = (bf16[4,64,2048]{2,1,0:T(8,128)(2,1)}, bf16[4,64,2048]{2,1,0:T(8,128)(2,1)S(1)}, u32[]{:S(2)}, u32[]{:S(2)}) collective-permute-start(bf16[4,64,2048]{2,1,0:T(8,128)(2,1)} %get-tuple-element.110), channel_id=1, source_target_pairs={{0,64},{1,65},{2,66},{3,67},{4,68},{5,69},{6,70},{7,71},{8,76},{9,... | collective-permute-start | bytes 3145736 | tf_op jit(solution)/shard_map/ppermute | solution.py:38
  177.9 24.2 %collective-permute-start.18 = (bf16[4,64,2048]{2,1,0:T(8,128)(2,1)}, bf16[4,64,2048]{2,1,0:T(8,128)(2,1)S(1)}, u32[]{:S(2)}, u32[]{:S(2)}) collective-permute-start(bf16[4,64,2048]{2,1,0:T(8,128)(2,1)} %copy-done.41), channel_id=1, source_target_pairs={{0,64},{1,65},{2,66},{3,67},{4,68},{5,69},{6,70},{7,71},{8,76},{9,... | collective-permute-start | bytes 3145736 | tf_op jit(solution)/shard_map/ppermute | solution.py:38
  202.8 16.9 %collective-permute-start.19 = (bf16[4,64,2048]{2,1,0:T(8,128)(2,1)S(1)}, bf16[4,64,2048]{2,1,0:T(8,128)(2,1)S(1)}, u32[]{:S(2)}, u32[]{:S(2)}) collective-permute-start(bf16[4,64,2048]{2,1,0:T(8,128)(2,1)S(1)} %get-tuple-element.129), channel_id=1, source_target_pairs={{0,64},{1,65},{2,66},{3,67},{4,68},{5,69},{6,70},{7,71},{8,76},{9,... | collective-permute-start | bytes 3145736 | tf_op jit(solution)/shard_map/ppermute | solution.py:38
  210.1 30.6 %collective-permute-start.17 = (bf16[320,1024]{1,0:T(8,128)(2,1)}, bf16[320,1024]{1,0:T(8,128)(2,1)}, u32[]{:S(2)}, u32[]{:S(2)}) collective-permute-start(bf16[320,1024]{1,0:T(8,128)(2,1)} %convolution_convert_fusion.2), channel_id=1, source_target_pairs={{0,8},{1,9},{2,10},{3,11},{4,12},{5,13},{6,14},{7,15},{8,0},{9,1},... | collective-permute-start | bytes 1966088 | tf_op jit(solution)/shard_map/ppermute | solution.py:38
  212.5 35.3 %collective-permute-start.16 = (bf16[320,1024]{1,0:T(8,128)(2,1)}, bf16[320,1024]{1,0:T(8,128)(2,1)}, u32[]{:S(2)}, u32[]{:S(2)}) collective-permute-start(bf16[320,1024]{1,0:T(8,128)(2,1)} %convolution_convert_fusion.4), channel_id=1, source_target_pairs={{0,8},{1,9},{2,10},{3,11},{4,12},{5,13},{6,14},{7,15},{8,0},{9,1},... | collective-permute-start | bytes 1966088 | tf_op jit(solution)/shard_map/ppermute | solution.py:38
  220.8 15.3 %all-to-all-start.2 = ((bf16[4,64,2048]{2,1,0:T(8,128)(2,1)}), bf16[4,64,2048]{2,1,0:T(8,128)(2,1)S(1)}, u32[]{:S(2)}, u32[]{:S(2)}) async-start(bf16[4,64,2048]{2,1,0:T(8,128)(2,1)} %get-tuple-element.131), calls=%async_computation.4 | async-start | bytes 2097152 | tf_op jit(solution)/shard_map/all_to_all | solution.py:649
  236.9 13.3 %all-to-all-start.3 = ((bf16[4,16,2048]{2,1,0:T(8,128)(2,1)}), bf16[4,16,2048]{2,1,0:T(8,128)(2,1)S(1)}, u32[]{:S(2)}, u32[]{:S(2)}) async-start(bf16[4,16,2048]{2,1,0:T(8,128)(2,1)} %bitcast.18), calls=%async_computation.5 | async-start | bytes 524288 | tf_op jit(solution)/shard_map/all_to_all | solution.py:649
  253.3 25.9 %all-to-all-start.4 = ((bf16[8,32,2176]{2,1,0:T(8,128)(2,1)}), bf16[8,32,2176]{2,1,0:T(8,128)(2,1)S(1)}, u32[]{:S(2)}, u32[]{:S(2)}) async-start(bf16[8,32,2176]{2,1,0:T(8,128)(2,1)} %join.1), calls=%async_computation.6 | async-start | bytes 2228224 | tf_op jit(solution)/shard_map/all_to_all | solution.py:649
  261.1 21.6 %collective-permute-start.21 = (bf16[32,1024]{1,0:T(8,128)(2,1)S(1)}, bf16[32,1024]{1,0:T(8,128)(2,1)S(1)}, u32[]{:S(2)}, u32[]{:S(2)}) collective-permute-start(bf16[32,1024]{1,0:T(8,128)(2,1)S(1)} %copy-done.44), channel_id=1, source_target_pairs={{0,64},{1,65},{2,66},{3,67},{4,68},{5,69},{6,70},{7,71},{8,72},{9,... | collective-permute-start | bytes 196616 | tf_op jit(solution)/shard_map/ppermute | solution.py:38
  279.8 4.6 %collective-permute-start.20 = (bf16[16,2048]{1,0:T(8,128)(2,1)S(1)}, bf16[16,2048]{1,0:T(8,128)(2,1)S(1)}, u32[]{:S(2)}, u32[]{:S(2)}) collective-permute-start(bf16[16,2048]{1,0:T(8,128)(2,1)S(1)} %get-tuple-element.133), channel_id=1, source_target_pairs={{0,64},{1,65},{2,66},{3,67},{4,68},{5,69},{6,70},{7,71},{8,72},{9,... | collective-permute-start | bytes 196616 | tf_op jit(solution)/shard_map/ppermute | solution.py:38
  309.7 6.4 %collective-permute-start.22 = (bf16[8,48,2176]{2,1,0:T(8,128)(2,1)S(1)}, bf16[8,48,2176]{2,1,0:T(8,128)(2,1)S(1)}, u32[]{:S(2)}, u32[]{:S(2)}) collective-permute-start(bf16[8,48,2176]{2,1,0:T(8,128)(2,1)S(1)} %all_to_all.31.refs_1_), channel_id=1, source_target_pairs={{0,8},{1,9},{2,10},{3,11},{4,12},{5,13},{6,14},{7,15},{8,0},{9,1},... | collective-permute-start | bytes 5013512 | tf_op jit(solution)/shard_map/ppermute | solution.py:38
  (65 other events, 656.2 us)
Sparse Core Ops, SparseCore 0:
  11.5 29.3 all-gather.5
  130.0 45.6 reduce-scatter.4
  178.2 46.5 reduce-scatter.2
Sparse Core Ops, SparseCore 1:
  56.6 47.9 all-gather.3
where the time goes:
time: 329 us; the launch traced here: 328 us
  Pallas kernels  89.6 us (27%)
  starting transfers between devices  67.9 us (21%)
  waiting for transfers between devices  64.7 us (20%)
  blocking collectives  46.2 us (14%)
  matrix products  19.5 us (6%)
  local copies, waits for them, and re-layouts  18.7 us (6%)
  between operations  16 us (5%)
  other arithmetic  5.18 us (2%)
    pallas_call x28, Pallas kernels, run(): call(*(in_hbm(a) if n in pinned else a for n, a in enumerate(args)), *(in...  89.6 us
    ppermute x23, starting transfers between devices, permute(): lax.ppermute(value, AXES, [(l, linear_of(*move(*place(l)))) for l in rang...  47.8 us
    all_to_all x2, blocking collectives, all_to_all(): lax.all_to_all(value, axis, 0, 0, tiled=True, axis_index_groups=groups)  46.2 us
    ppermute x23, waiting for transfers between devices, permute(): lax.ppermute(value, AXES, [(l, linear_of(*move(*place(l)))) for l in rang...  44.5 us
    all_to_all x4, starting transfers between devices, all_to_all(): lax.all_to_all(value, axis, 0, 0, tiled=True, axis_index_groups=groups)  19.9 us
    all_to_all x4, waiting for transfers between devices, all_to_all(): lax.all_to_all(value, axis, 0, 0, tiled=True, axis_index_groups=groups)  19.2 us
    unnamed x132, local copies, waits for them, and re-layouts  17.3 us
    dot_general x4, matrix products, dot_nt(): lax.dot_general(left, right, (((1,), (1,)), ((), ())), preferred_element_...  10.2 us
  transfers between devices with their start and end apart: 31, of which 14 were waited for; matrix products, arithmetic and copies ran while one was open for 7% of the time, Pallas kernels for 19%

commit v1 on v0

--- a/solution.py
+++ b/solution.py
@@ -449,37 +449,44 @@
 
 
 def grad_fc1_kernel(table, left, right, *refs):
-    outs = refs[:4]
+    along_y, along_x = refs[:4], refs[4:8]
     terms = dot_tn(left[...], right[...]).astype(BF)
-    hi = lax.rem(pl.program_id(0), 2)
-    for n, out in enumerate(outs):
-        y = source_in(table, Y, n + 1)
-        for lo in range(2):
-
-            @pl.when(y == hi * 2 + lo)
+    hi, pair = lax.rem(pl.program_id(0), 2), pl.program_id(0) // 2
+    for n in range(4):
+        y, x = source_in(table, Y, n + 1), source_in(table, X, n + 1)
+        for e in range(2):
+
+            @pl.when(y == hi * 2 + e)
             def _():
-                for x in range(2):
-                    at = (2 * x + lo) * 64
-                    out[x] = terms[at : at + 64]
+                for k in range(2):
+                    at = (2 * k + e) * 64
+                    along_y[n][k] = terms[at : at + 64, :1024]
+
+            @pl.when(x == pair * 2 + e)
+            def _():
+                along_x[n][hi] = terms[e * 128 : (e + 1) * 128, 1024:]
 
 
 def grad_fc1_terms(here, normed, d_pre, late):
     m = normed.shape[0]
-    return kernel_call(
+    results = kernel_call(
         grad_fc1_kernel,
         "grad_fc1",
-        [struct((4, 64, 2048), BF)] * 4 + [TOKEN],
+        [struct((4, 64, 1024), BF)] * 4 + [struct((2, 128, 1024), BF)] * 4 + [TOKEN],
         us=5,
         late=late,
-        pinned_out=range(4),
+        pinned_out=range(8),
         grid=(4,),
         in_specs=[
             SMEM,
             pl.BlockSpec((m, 256), lambda i: (0, lax.rem(i, 2) * 2 + i // 2)),
             pl.BlockSpec((m, 2048), lambda i: (0, 0)),
         ],
-        out_specs=[pl.BlockSpec((2, 64, 2048), lambda i: (i // 2, 0, 0))] * 4 + [TOKEN_SPEC],
+        out_specs=[pl.BlockSpec((2, 64, 1024), lambda i: (i // 2, 0, 0))] * 4
+        + [pl.BlockSpec((2, 128, 1024), lambda i: (0, 0, 0))] * 4
+        + [TOKEN_SPEC],
     )(here.table, normed, d_pre)
+    return results[:4], results[4:8], results[8]
 
 
 def grad_qkv_kernel(normed, d_packed, mixed, d_attended, out):
@@ -523,39 +530,136 @@
     return total
 
 
-def sum_kernel(*refs):
-    refs[-1][...] = total_of(refs[:-1]).astype(BF)
-
-
-def sum_of(name, blocks, late=()):
-    block = pl.BlockSpec((2,) + blocks[0].shape[1:], lambda i: (i, 0, 0))
-    return kernel_call(
-        lambda *refs: sum_kernel(*refs[:-1]),
-        name,
-        [struct(blocks[0].shape, BF), TOKEN],
-        us=2,
+def fc2_split_kernel(table, blocks, *outs):
+    for r, out in enumerate(outs[:4]):
+        x = place_in(table, X, r)
+        for hi in range(2):
+            out[hi] = blocks[hi * 4 + x]
+
+
+def fc2_split(here, blocks):
+    return kernel_call(
+        fc2_split_kernel,
+        "fc2_split",
+        [struct((2, 64, 1024), BF)] * 4 + [TOKEN],
+        us=1,
+        grid=(1,),
+        in_specs=[SMEM, pl.BlockSpec((8, 64, 1024), lambda i: (0, 0, 0))],
+        out_specs=[pl.BlockSpec((2, 64, 1024), lambda i: (0, 0, 0))] * 4 + [TOKEN_SPEC],
+    )(here.table, blocks)
+
+
+def fc2_sum_kernel(table, *refs):
+    ins, (kept, sent) = refs[:4], refs[4:]
+    total = total_of(ins)
+    kept[...] = jnp.where(table[HI] == 0, total[0], total[1])
+    sent[...] = jnp.where(table[HI] == 0, total[1], total[0]).astype(BF)
+
+
+def fc2_add_kernel(table, own, arrived, kept, sent):
+    total = own[...] + arrived[...].astype(F32)
+    low, high = total[:32], total[32:]
+    kept[...] = jnp.where(table[LO] == 0, low, high)
+    sent[...] = jnp.where(table[LO] == 0, high, low).astype(BF)
+
+
+def fc2_sums(here, blocks):
+    block = pl.BlockSpec((2, 64, 1024), lambda i: (0, 0, 0))
+    half = pl.BlockSpec((64, 1024), lambda i: (0, 0))
+    part = pl.BlockSpec((32, 1024), lambda i: (0, 0))
+    kept, sent = kernel_call(
+        fc2_sum_kernel,
+        "fc2_sum",
+        [struct((64, 1024), F32), struct((64, 1024), BF)],
+        us=1,
+        grid=(1,),
+        in_specs=[SMEM] + [block] * 4,
+        out_specs=[half, half],
+    )(here.table, *blocks)
+    kept, sent = kernel_call(
+        fc2_add_kernel,
+        "fc2_add",
+        [struct((32, 1024), F32), struct((32, 1024), BF)],
+        us=1,
+        grid=(1,),
+        in_specs=[SMEM, half, half],
+        out_specs=[part, part],
+    )(here.table, kept, permute(sent, flip_hi))
+    return kept, permute(sent, flip_lo)
+
+
+def add_kernel(y, y_terms, x, x_terms, y_out, x_out, done):
+    y_out[...] = total_of((y, y_terms)).astype(BF)
+    x_out[...] = total_of((x, x_terms)).astype(BF)
+
+
+def add_both(arrived, terms, late=()):
+    y = pl.BlockSpec((2, 64, 1024), lambda i: (i, 0, 0))
+    x = pl.BlockSpec((1, 128, 1024), lambda i: (i, 0, 0))
+    *sums, done = kernel_call(
+        add_kernel,
+        "fc1_add",
+        [struct((4, 64, 1024), BF), struct((2, 128, 1024), BF), TOKEN],
+        us=1,
         late=late,
         grid=(2,),
-        in_specs=[block] * len(blocks),
-        out_specs=[block, TOKEN_SPEC],
-    )(*blocks)
-
-
-def sum_first_kernel(blocks, out):
-    out[...] = jnp.sum(blocks[...].astype(F32), axis=0).astype(BF)
-
-
-def sum_first(name, blocks):
-    k, r, n = blocks.shape
-    return kernel_call(
-        sum_first_kernel,
-        name,
-        struct((r, n), BF),
+        in_specs=[y, y, x, x],
+        out_specs=[y, x, TOKEN_SPEC],
+    )(arrived[0], terms[0], arrived[1], terms[1])
+    return sums, done
+
+
+def ring_both(sums):
+    return [permute(v, ring_move(axis)) for v, axis in zip(sums, "yx")]
+
+
+def last_kernel(table, y, y_terms, x, x_terms, y_out, kept, sent):
+    y_out[...] = total_of((y, y_terms)).astype(BF)
+    total = total_of((x, x_terms))
+    kept[...] = jnp.where(table[HI] == 0, total[0], total[1])
+    sent[...] = jnp.where(table[HI] == 0, total[1], total[0]).astype(BF)
+
+
+def last_both(here, arrived, terms, late):
+    y = pl.BlockSpec((4, 64, 1024), lambda i: (0, 0, 0))
+    x = pl.BlockSpec((2, 128, 1024), lambda i: (0, 0, 0))
+    half = pl.BlockSpec((128, 1024), lambda i: (0, 0))
+    return kernel_call(
+        last_kernel,
+        "fc1_last",
+        [struct((4, 64, 1024), BF), struct((128, 1024), F32), struct((128, 1024), BF)],
+        us=1,
+        late=late,
+        grid=(1,),
+        in_specs=[SMEM, y, y, x, x],
+        out_specs=[y, half, half],
+    )(here.table, arrived[0], terms[0], arrived[1], terms[1])
+
+
+def slices_kernel(table, y_blocks, x_kept, x_sent, out):
+    y_sum = jnp.sum(y_blocks[...].astype(F32), axis=0).astype(BF)
+    x_sum = (x_kept[...] + x_sent[...].astype(F32)).astype(BF)
+    for k in range(8):
+        z, lo = k // 2, k % 2
+        rows = y_sum[z * 16 : (z + 1) * 16]
+        out[k, :, :1024] = jnp.where(table[LO] == lo, rows, jnp.zeros_like(rows))
+        at = lo * 64 + z * 16
+        out[k, :, 1024:] = x_sum[at : at + 16]
+
+
+def fc1_slices(here, y_blocks, x_kept, x_sent):
+    def whole(*shape):
+        return pl.BlockSpec(shape, lambda i: (0,) * len(shape))
+
+    return kernel_call(
+        slices_kernel,
+        "fc1_slices",
+        struct((8, 16, 2048), BF),
         us=1,
         grid=(1,),
-        in_specs=[pl.BlockSpec((k, r, n), lambda i: (0, 0, 0))],
-        out_specs=pl.BlockSpec((r, n), lambda i: (0, 0)),
-    )(blocks)
+        in_specs=[SMEM, whole(4, 64, 1024), whole(128, 1024), whole(128, 1024)],
+        out_specs=whole(8, 16, 2048),
+    )(here.table, y_blocks, x_kept, x_sent)
 
 
 def join_kernel(qkv, vectors, out):
@@ -1129,7 +1233,8 @@
     d_pre, fc1_bias_sum = hidden_back(d_branch, fc2_all, slope, (fc2_done,))
     d_normed_two = dot_nt(d_pre, fc1_all).astype(BF)
     *grad_fc1, fc1_done = grad_fc1_terms(here, normed_two, d_pre, (d_normed_two,))
-    fc1_arrived = permute(grad_fc1[0], ring_move("y"))
+    grad_fc1 = list(zip(*grad_fc1))
+    fc1_arrived = ring_both(grad_fc1[0])
     d_middle, d_attended, middle_sums = middle_back(
         shares,
         d_normed_two,
@@ -1141,11 +1246,13 @@
         (fc1_done,),
     )
     d_mixed = dot_nt(d_attended, out_all).astype(BF)
+    fc1_sum, add_done = add_both(fc1_arrived, grad_fc1[1], (middle_sums,))
+    fc1_arrived = ring_both(fc1_sum)
     d_packed, packed_sums = attention_back(
-        packed, query_shift, value_shift, blocked, d_mixed, ()
-    )
-    fc1_sum, add_done = sum_of("fc1_add", (fc1_arrived, grad_fc1[1]), (packed_sums,))
-    fc1_arrived = permute(fc1_sum, ring_move("y"))
+        packed, query_shift, value_shift, blocked, d_mixed, (add_done,)
+    )
+    fc1_sum, add_done = add_both(fc1_arrived, grad_fc1[2], (packed_sums,))
+    fc1_arrived = ring_both(fc1_sum)
     grad_qkv = grad_qkv_terms(normed, d_packed, mixed, d_attended, (add_done,))
     grad_qkv, d_packed, hidden = lax.optimization_barrier((grad_qkv, d_packed, hidden))
     qkv_sum = lax.psum_scatter(
@@ -1155,14 +1262,13 @@
         axis_index_groups=Z_GROUPS,
         tiled=True,
     ).reshape(8, 32, 2048)
-    fc2_sum = all_to_all(fc2_sum.reshape(8, 64, 1024), "fsdp")
-    fc2_kept, fc2_sent, _ = sum_and_halve(here, "fc2_lo", fc2_sum, 1024)
-    fc1_sum, _ = sum_of("fc1_add", (fc1_arrived, grad_fc1[2]), (fc2_kept,))
-    fc1_arrived = permute(fc1_sum, ring_move("y"))
-    fc1_sum, _ = sum_of("fc1_add", (fc1_arrived, grad_fc1[3]))
-    fc1_sum = all_to_all(fc1_sum, "fsdp", X_GROUPS)
-    fc1_sum = sum_first("fc1_sum", fc1_sum).reshape(4, 16, 2048)
-    fc1_sum = all_to_all(fc1_sum, "dp", Z_GROUPS)
+    *fc2_blocks, split_done = fc2_split(here, fc2_sum.reshape(8, 64, 1024))
+    fc2_kept, fc2_sent = fc2_sums(here, exchange(fc2_blocks, "x"))
+    y_sum, x_kept, x_sent = last_both(here, fc1_arrived, grad_fc1[3], (split_done,))
+    fc1_sum = fc1_slices(
+        here, all_to_all(y_sum, "fsdp", X_GROUPS), x_kept, permute(x_sent, flip_hi)
+    )
+    fc1_sum = all_to_all(fc1_sum, "dp", SLICE_GROUPS)
 
     d_normed_sent = permute(dot_nt(d_packed[own_rows:], qkv_all).astype(BF), swap_core)
     d_normed_own = dot_nt(d_packed[:own_rows], qkv_all).astype(BF)

time: 329 us -> 309 us (0.939)
  blocking collectives: 46.2 us -> 22.5 us
  waiting for transfers between devices: 64.7 us -> 56.2 us
  matrix products: 19.5 us -> 24.1 us
  Pallas kernels: 89.6 us -> 93.8 us
    all_to_all x2 -> x1, blocking collectives: 46.2 us -> 22.5 us  [all_to_all(): lax.all_to_all(value, axis, 0, 0, tiled=True, axis_index_groups=groups)]
    ppermute x23 -> x31, waiting for transfers between devices: 44.5 us -> 37.5 us  [permute(): lax.ppermute(value, AXES, [(l, linear_of(*move(*place(l)))) for l in rang...]
    pallas_call x28 -> x30, Pallas kernels: 89.6 us -> 93.8 us  [run(): call(*(in_hbm(a) if n in pinned else a for n, a in enumerate(args)), *(in...]
    ppermute x23 -> x31, starting transfers between devices: 47.8 us -> 51.6 us  [permute(): lax.ppermute(value, AXES, [(l, linear_of(*move(*place(l)))) for l in rang...]
    all_to_all x4, starting transfers between devices: 19.9 us -> 16.6 us  [all_to_all(): lax.all_to_all(value, axis, 0, 0, tiled=True, axis_index_groups=groups)]
    unnamed x132 -> x126, local copies, waits for them, and re-layouts: 17.3 us -> 20 us
  transfers between devices with their start and end apart: 31 -> 39, of which waited for: 14 -> 11; matrix products, arithmetic and copies ran while one was open for 7% -> 9% of each run, Pallas kernels for 19% -> 22%
where the time goes in v1:
time: 309 us; the launch traced here: 308 us
  Pallas kernels  93.8 us (30%)
  starting transfers between devices  68.3 us (22%)
  waiting for transfers between devices  56.2 us (18%)
  matrix products  24.1 us (8%)
  blocking collectives  22.5 us (7%)
  local copies, waits for them, and re-layouts  21.4 us (7%)
  between operations  16.1 us (5%)
  other arithmetic  5.18 us (2%)
    pallas_call x30, Pallas kernels, run(): call(*(in_hbm(a) if n in pinned else a for n, a in enumerate(args)), *(in...  93.8 us
    ppermute x31, starting transfers between devices, permute(): lax.ppermute(value, AXES, [(l, linear_of(*move(*place(l)))) for l in rang...  51.6 us
    ppermute x31, waiting for transfers between devices, permute(): lax.ppermute(value, AXES, [(l, linear_of(*move(*place(l)))) for l in rang...  37.5 us
    all_to_all x1, blocking collectives, all_to_all(): lax.all_to_all(value, axis, 0, 0, tiled=True, axis_index_groups=groups)  22.5 us
    unnamed x126, local copies, waits for them, and re-layouts  20 us
    all_to_all x4, waiting for transfers between devices, all_to_all(): lax.all_to_all(value, axis, 0, 0, tiled=True, axis_index_groups=groups)  17.7 us
    all_to_all x4, starting transfers between devices, all_to_all(): lax.all_to_all(value, axis, 0, 0, tiled=True, axis_index_groups=groups)  16.6 us
    dot_general x4, matrix products, dot(): return jnp.dot(left, right, preferred_element_type=F32)  12.1 us
  transfers between devices with their start and end apart: 39, of which 11 were waited for; matrix products, arithmetic and copies ran while one was open for 9% of the time, Pallas kernels for 22%

profile of v1, /device:TPU:1, one launch (start us, length us, event | category | flops | bytes accessed | tf_op | source)
XLA Modules:
  0.0 307.6 jit_solution(4488892350028363719)
XLA Ops:
  8.2 3.1 %prepare.1 = (bf16[8,32,1664]{2,1,0:T(8,128)(2,1)}, bf16[64,2048]{1,0:T(8,128)(2,1)}, bf16[256,1024]{1,0:T(8,128)(2,1)S(1)}, bf16[64,1024]{1,0:T(8,128)(2,1)}) custom-call(s32[6]{0:T(128)S(1)} %stack.33.refs_0_, bf16[128,3072]{1,0:T(8,128)(2,1)} %refs_1_.1, bf16[128,4096]{1,0:T(8,128)(2,1)} %refs_2_.3, bf16[512,1024]{1,0:T(8,128)(2,1)} %refs_3_.1, ...), custom_call_target="tpu_custom_call" | custom-call | flops 862499968 | bytes 65536 | tf_op jit(solution)/shard_map/prepare/pallas_call | solution.py:186
  11.4 3.6 %collective-permute-start.6 = (bf16[256,1024]{1,0:T(8,128)(2,1)S(1)}, bf16[256,1024]{1,0:T(8,128)(2,1)}, u32[]{:S(2)}, u32[]{:S(2)}) collective-permute-start(bf16[256,1024]{1,0:T(8,128)(2,1)S(1)} %get-tuple-element.102.refs_1_), channel_id=1, source_target_pairs={{0,68},{1,69},{2,70},{3,71},{4,64},{5,65},{6,66},{7,67},{8,76},{9,... | collective-permute-start | bytes 1572872 | tf_op jit(solution)/shard_map/ppermute | solution.py:38
  15.0 4.2 %all-to-all-start = ((bf16[8,32,1664]{2,1,0:T(8,128)(2,1)}), bf16[8,32,1664]{2,1,0:T(8,128)(2,1)S(1)}, u32[]{:S(2)}, u32[]{:S(2)}) async-start(bf16[8,32,1664]{2,1,0:T(8,128)(2,1)} %get-tuple-element.99), calls=%async_computation | async-start | bytes 1703936 | tf_op jit(solution)/shard_map/all_to_all | solution.py:753
  19.3 15.2 %collective-permute-done.6.refs_2_ = bf16[256,1024]{1,0:T(8,128)(2,1)} collective-permute-done((bf16[256,1024]{1,0:T(8,128)(2,1)S(1)}, bf16[256,1024]{1,0:T(8,128)(2,1)}, u32[]{:S(2)}, u32[]{:S(2)}) %collective-permute-start.6) | collective-permute-done | bytes 524320 | tf_op jit(solution)/shard_map/ppermute | solution.py:38
  36.2 3.7 %collective-permute-start.7 = (bf16[2,256,1024]{2,1,0:T(8,128)(2,1)S(1)}, bf16[2,256,1024]{2,1,0:T(8,128)(2,1)}, u32[]{:S(2)}, u32[]{:S(2)}) collective-permute-start(bf16[2,256,1024]{2,1,0:T(8,128)(2,1)S(1)} %fc2_hi.1.refs_1_), channel_id=1, source_target_pairs={{0,1},{1,2},{2,3},{3,0},{4,5},{5,6},{6,7},{7,4},{8,11},{9,8},{10,9... | collective-permute-start | bytes 3145736 | tf_op jit(solution)/shard_map/ppermute | solution.py:38
  43.1 4.1 %collective-permute-start.3 = (bf16[8,32,1664]{2,1,0:T(8,128)(2,1)S(1)}, bf16[8,32,1664]{2,1,0:T(8,128)(2,1)}, u32[]{:S(2)}, u32[]{:S(2)}) collective-permute-start(bf16[8,32,1664]{2,1,0:T(8,128)(2,1)S(1)} %all-to-all-done.refs_1_), channel_id=1, source_target_pairs={{0,16},{1,17},{2,18},{3,19},{4,20},{5,21},{6,22},{7,23},{8,56},{9,... | collective-permute-start | bytes 2555912 | tf_op jit(solution)/shard_map/ppermute | solution.py:38
  47.2 4.5 %collective-permute-done.7.refs_2_ = bf16[2,256,1024]{2,1,0:T(8,128)(2,1)} collective-permute-done((bf16[2,256,1024]{2,1,0:T(8,128)(2,1)S(1)}, bf16[2,256,1024]{2,1,0:T(8,128)(2,1)}, u32[]{:S(2)}, u32[]{:S(2)}) %collective-permute-start.7) | collective-permute-done | bytes 1048608 | tf_op jit(solution)/shard_map/ppermute | solution.py:38
  51.7 3.5 %collective-permute-start.8 = (bf16[2,256,1024]{2,1,0:T(8,128)(2,1)}, bf16[2,256,1024]{2,1,0:T(8,128)(2,1)}, u32[]{:S(2)}, u32[]{:S(2)}) collective-permute-start(bf16[2,256,1024]{2,1,0:T(8,128)(2,1)} %collective-permute-done.7.refs_2_), channel_id=1, source_target_pairs={{0,1},{1,2},{2,3},{3,0},{4,5},{5,6},{6,7},{7,4},{8,11},{9,8},{10,9... | collective-permute-start | bytes 3145736 | tf_op jit(solution)/shard_map/ppermute | solution.py:38
  56.8 3.5 %collective-permute-start.4 = (bf16[8,32,1664]{2,1,0:T(8,128)(2,1)}, bf16[8,32,1664]{2,1,0:T(8,128)(2,1)}, u32[]{:S(2)}, u32[]{:S(2)}) collective-permute-start(bf16[8,32,1664]{2,1,0:T(8,128)(2,1)} %collective-permute-done.3.refs_2_), channel_id=1, source_target_pairs={{0,16},{1,17},{2,18},{3,19},{4,20},{5,21},{6,22},{7,23},{8,56},{9,... | collective-permute-start | bytes 2555912 | tf_op jit(solution)/shard_map/ppermute | solution.py:38
  69.9 3.4 %compact.1 = (bf16[640,1024]{1,0:T(8,128)(2,1)S(1)}, bf16[640,1024]{1,0:T(8,128)(2,1)S(1)}, bf16[640,1024]{1,0:T(8,128)(2,1)S(1)}, f32[640,1]{1,0:T(8,128)S(1)}, f32[4,160,160]{2,1,0:T(8,128)S(1)}) custom-call(s32[2]{0:T(128)S(1)} %get-tuple-element.182.refs_0_, f32[2]{0:T(128)S(1)} %get-tuple-element.181.refs_1_.refs_0_, bf16[384,1024]{1,0:T(8,128)(2,1)S(1)} %copy-done.22, ...), custom_call_target="tpu_custom_call" | custom-call | flops 1437500032 | bytes 65536 | tf_op jit(solution)/shard_map/compact/pallas_call | solution.py:186
  80.8 9.0 %collective-permute-done.5.refs_4_ = bf16[8,32,1664]{2,1,0:T(8,128)(2,1)S(1)} collective-permute-done((bf16[8,32,1664]{2,1,0:T(8,128)(2,1)}, bf16[8,32,1664]{2,1,0:T(8,128)(2,1)S(1)}, u32[]{:S(2)}, u32[]{:S(2)}) %collective-permute-start.5) | collective-permute-done | bytes 852000 | tf_op jit(solution)/shard_map/ppermute | solution.py:38
  98.9 5.0 %attention.1 = (bf16[640,512]{1,0:T(8,128)(2,1)S(1)}, f32[8,128]{1,0:T(8,128)S(1)}) custom-call(f32[640,1536]{1,0:T(8,128)S(1)} %fusion.13.refs_0_, f32[1,512]{1,0:T(1,128)S(1)} %get-tuple-element.103.refs_1_, f32[1,512]{1,0:T(1,128)S(1)} %get-tuple-element.104.refs_2_, f32[4,160,160]{2,1,0:T(8,128)S(1)} %get-tuple-element.105.refs_3_, ...), custom_call_target="tpu_custom_call" | custom-call | flops 1437500032 | bytes 65536 | tf_op jit(solution)/shard_map/attention/pallas_call | solution.py:186
  112.3 3.2 %middle_layer.1 = (f32[640,1024]{1,0:T(8,128)}, bf16[640,1024]{1,0:T(8,128)(2,1)S(1)}) custom-call(bf16[640,1024]{1,0:T(8,128)(2,1)S(1)} %convolution_convert_fusion.1.refs_0_, bf16[640,1024]{1,0:T(8,128)(2,1)S(1)} %collective-permute-done.13.refs_1_, bf16[640,1024]{1,0:T(8,128)(2,1)S(1)} %get-tuple-element.98.refs_2_.refs_4_, f32[640,1]{1,0:T(8,128)S(1)} %copy-done.39, ...), custom_call_target="tpu_custom_call" | custom-call | flops 1724999936 | bytes 65536 | tf_op jit(solution)/shard_map/middle_layer/pallas_call | solution.py:186
  115.5 8.7 %hidden_layer.1 = (bf16[640,2048]{1,0:T(8,128)(2,1)S(1)}, bf16[640,2048]{1,0:T(8,128)(2,1)S(1)}) custom-call(bf16[640,1024]{1,0:T(8,128)(2,1)S(1)} %get-tuple-element.115.refs_0_.refs_1_, bf16[1024,2048]{1,0:T(8,128)(2,1)S(1)} %bitcast.44, f32[1,2048]{1,0:T(1,128)S(1)} %get-tuple-element.116.refs_2_), custom_call_target="tpu_custom_call" | custom-call | flops 3162500096 | bytes 65536 | tf_op jit(solution)/shard_map/hidden_layer/pallas_call | solution.py:186
  124.3 5.6 %grad_fc2.1 = (bf16[4,8,64,1024]{3,2,1,0:T(8,128)(2,1)}, f32[8,128]{1,0:T(8,128)S(1)}) custom-call(bf16[640,2048]{1,0:T(8,128)(2,1)S(1)} %get-tuple-element.138.refs_0_, bf16[640,1024]{1,0:T(8,128)(2,1)S(1)} %copy-done.17), custom_call_target="tpu_custom_call" | custom-call | flops 1437500032 | bytes 65536 | tf_op jit(solution)/shard_map/grad_fc2/pallas_call | solution.py:186
  133.4 5.1 %hidden_back.1 = (bf16[640,2048]{1,0:T(8,128)(2,1)S(1)}, f32[1,2048]{1,0:T(1,128)S(1)}) custom-call(bf16[640,1024]{1,0:T(8,128)(2,1)S(1)} %copy-done.18, bf16[2048,1024]{1,0:T(8,128)(2,1)S(1)} %bitcast.41, bf16[640,2048]{1,0:T(8,128)(2,1)S(1)} %copy-done.11, f32[8,128]{1,0:T(8,128)S(1)} %get-tuple-element.119.refs_3_), custom_call_target="tpu_custom_call" | custom-call | flops 1724999936 | bytes 65536 | tf_op jit(solution)/shard_map/hidden_back/pallas_call | solution.py:186
  142.5 7.4 %grad_fc1.1 = (bf16[4,64,1024]{2,1,0:T(8,128)(2,1)}, bf16[4,64,1024]{2,1,0:T(8,128)(2,1)}, bf16[4,64,1024]{2,1,0:T(8,128)(2,1)}, bf16[4,64,1024]{2,1,0:T(8,128)(...) custom-call(s32[6]{0:T(128)S(1)} %stack.33.refs_0_, ...), custom_call_target="tpu_custom_call" | custom-call | flops 1437500032 | bytes 65536 | tf_op jit(solution)/shard_map/grad_fc1/pallas_call | solution.py:186
  157.1 5.0 %middle_back.1 = (f32[640,1024]{1,0:T(8,128)S(1)}, bf16[640,1024]{1,0:T(8,128)(2,1)S(1)}, f32[8,1024]{1,0:T(8,128)S(1)}) custom-call(f32[2]{0:T(128)S(1)} %get-tuple-element.181.refs_1_.refs_0_, bf16[640,1024]{1,0:T(8,128)(2,1)S(1)} %copy-done.45, bf16[640,1024]{1,0:T(8,128)(2,1)S(1)} %collective-permute-done.14.refs_2_, ...), custom_call_target="tpu_custom_call" | custom-call | flops 2012499968 | bytes 65536 | tf_op jit(solution)/shard_map/middle_back/pallas_call | solution.py:186
  167.2 10.4 %attention_back.1 = (bf16[640,1536]{1,0:T(8,128)(2,1)S(1)}, f32[1,1536]{1,0:T(1,128)S(1)}) custom-call(f32[640,1536]{1,0:T(8,128)S(1)} %copy-done.7, f32[1,512]{1,0:T(1,128)S(1)} %get-tuple-element.103.refs_1_, f32[1,512]{1,0:T(1,128)S(1)} %get-tuple-element.104.refs_2_, f32[4,160,160]{2,1,0:T(8,128)S(1)} %copy-done.28, ...), custom_call_target="tpu_custom_call" | custom-call | flops 4600000000 | bytes 65536 | tf_op jit(solution)/shard_map/attention_back/pallas_call | solution.py:186
  179.0 5.4 %grad_qkv.1 = bf16[4,8,32,2048]{3,2,1,0:T(8,128)(2,1)} custom-call(bf16[640,1024]{1,0:T(8,128)(2,1)S(1)} %fusion.5.refs_0_, bf16[640,1536]{1,0:T(8,128)(2,1)S(1)} %get-tuple-element.141.refs_1_, bf16[640,512]{1,0:T(8,128)(2,1)S(1)} %copy-done.26, bf16[640,1024]{1,0:T(8,128)(2,1)S(1)} %get-tuple-element.124.refs_3_, f32[8,128]{1,0:T(8,128)S(1)} %get-tuple-element.137.refs_4_), custom_call_target="tpu_custom_call" | custom-call | flops 1437500032 | bytes 65536 | tf_op jit(solution)/shard_map/grad_qkv/pallas_call | solution.py:186
  185.5 4.7 %convolution_convert_fusion.2 = bf16[320,1024]{1,0:T(8,128)(2,1)} fusion(bf16[1024,1536]{1,0:T(8,128)(2,1)} %bitcast.47, bf16[640,1536]{1,0:T(8,128)(2,1)} %copy-done.15), kind=kOutput, calls=%fused_computation.10 | convolution fusion | flops 1006960640 | bytes 4784128 | tf_op jit(solution)/shard_map/dot_general | solution.py:951
  201.7 3.7 %all-to-all-start.1 = ((bf16[4,64,1024]{2,1,0:T(8,128)(2,1)}), bf16[4,64,1024]{2,1,0:T(8,128)(2,1)S(1)}, u32[]{:S(2)}, u32[]{:S(2)}) async-start(bf16[4,64,1024]{2,1,0:T(8,128)(2,1)} %copy-done.33), calls=%async_computation.3 | async-start | bytes 1048576 | tf_op jit(solution)/shard_map/all_to_all | solution.py:753
  205.6 5.3 %fusion.7.refs_1_ = f32[320,1024]{1,0:T(8,128)} fusion(bf16[2048,1024]{1,0:T(8,128)(2,1)} %bitcast.42, bf16[640,2048]{1,0:T(8,128)(2,1)} %copy-done.54), kind=kOutput, calls=%fused_computation.15 | convolution fusion | flops 1342177280 | bytes 6815744 | tf_op jit(solution)/shard_map/dot_general | solution.py:947
  217.8 3.8 %all-to-all-start.2 = ((bf16[8,16,2048]{2,1,0:T(8,128)(2,1)}), bf16[8,16,2048]{2,1,0:T(8,128)(2,1)S(1)}, u32[]{:S(2)}, u32[]{:S(2)}) async-start(bf16[8,16,2048]{2,1,0:T(8,128)(2,1)} %fc1_slices.1), calls=%async_computation.4 | async-start | bytes 1048576 | tf_op jit(solution)/shard_map/all_to_all | solution.py:753
  221.6 3.6 %convolution_convert_fusion.3.refs_2_ = bf16[320,1024]{1,0:T(8,128)(2,1)S(1)} fusion(bf16[1024,1536]{1,0:T(8,128)(2,1)} %bitcast.48, bf16[640,1536]{1,0:T(8,128)(2,1)} %copy-done.15), kind=kOutput, calls=%fused_computation.11 | convolution fusion | flops 1006960640 | bytes 4784128 | tf_op jit(solution)/shard_map/dot_general | solution.py:951
  225.2 3.6 %input_back.1 = (bf16[384,1024]{1,0:T(8,128)(2,1)}, f32[8,1024]{1,0:T(8,128)S(1)}) custom-call(s32[2]{0:T(128)S(1)} %get-tuple-element.182.refs_0_, f32[2]{0:T(128)S(1)} %get-tuple-element.181.refs_1_.refs_0_, bf16[320,1024]{1,0:T(8,128)(2,1)S(1)} %convolution_convert_fusion.3.refs_2_, bf16[320,1024]{1,0:T(8,128)(2,1)} %collective-permute-done.20.refs_3_, ...), custom_call_target="tpu_custom_call" | custom-call | flops 1150000000 | bytes 65536 | tf_op jit(solution)/shard_map/input_back/pallas_call | solution.py:186
  239.1 4.9 %all-to-all-start.3 = ((bf16[8,32,2176]{2,1,0:T(8,128)(2,1)}), bf16[8,32,2176]{2,1,0:T(8,128)(2,1)S(1)}, u32[]{:S(2)}, u32[]{:S(2)}) async-start(bf16[8,32,2176]{2,1,0:T(8,128)(2,1)} %join.1), calls=%async_computation.5 | async-start | bytes 2228224 | tf_op jit(solution)/shard_map/all_to_all | solution.py:753
  244.3 17.7 %all-to-all-done.3.refs_1_ = bf16[8,32,2176]{2,1,0:T(8,128)(2,1)S(1)} async-done(((bf16[8,32,2176]{2,1,0:T(8,128)(2,1)}), bf16[8,32,2176]{2,1,0:T(8,128)(2,1)S(1)}, u32[]{:S(2)}, u32[]{:S(2)}) %all-to-all-start.3) | async-done | bytes 1114144 | tf_op jit(solution)/shard_map/all_to_all | solution.py:753
  266.9 22.5 %all_to_all.25.refs_1_ = bf16[8,48,2176]{2,1,0:T(8,128)(2,1)S(1)} all-to-all(bf16[8,48,2176]{2,1,0:T(8,128)(2,1)S(1)} %pack.1), channel_id=1, replica_groups={{0,64,16,80,32,96,48,112},{8,72,24,88,40,104,56,120},{1,65,17,81,33,97,..., dimensions={0} | all-to-all | bytes 3342336 | tf_op jit(solution)/shard_map/all_to_all | solution.py:753
  289.4 3.4 %collective-permute-start.30 = (bf16[8,48,2176]{2,1,0:T(8,128)(2,1)S(1)}, bf16[8,48,2176]{2,1,0:T(8,128)(2,1)S(1)}, u32[]{:S(2)}, u32[]{:S(2)}) collective-permute-start(bf16[8,48,2176]{2,1,0:T(8,128)(2,1)S(1)} %all_to_all.25.refs_1_), channel_id=1, source_target_pairs={{0,8},{1,9},{2,10},{3,11},{4,12},{5,13},{6,14},{7,15},{8,0},{9,1},... | collective-permute-start | bytes 5013512 | tf_op jit(solution)/shard_map/ppermute | solution.py:38
  292.8 3.2 %collective-permute-done.30.refs_2_ = bf16[8,48,2176]{2,1,0:T(8,128)(2,1)S(1)} collective-permute-done((bf16[8,48,2176]{2,1,0:T(8,128)(2,1)S(1)}, bf16[8,48,2176]{2,1,0:T(8,128)(2,1)S(1)}, u32[]{:S(2)}, u32[]{:S(2)}) %collective-permute-start.30) | collective-permute-done | bytes 1671200 | tf_op jit(solution)/shard_map/ppermute | solution.py:38
  296.0 4.5 %unpack.1 = (f32[128,3072]{1,0:T(8,128)}, f32[2,8,8,1024]{3,2,1,0:T(8,128)}, f32[128,4096]{1,0:T(8,128)}, f32[2,8,32,1024]{3,2,1,0:T(8,128)}, f32[1,128]{1,0:T(1...) custom-call(s32[6]{0:T(128)S(1)} %stack.33.refs_0_, ...), custom_call_target="tpu_custom_call" | custom-call | flops 1437500032 | bytes 65536 | tf_op jit(solution)/shard_map/unpack/pallas_call | solution.py:186
  (228 shorter events, 97.2 us)
Async XLA Ops:
  8.0 32.9 %all-gather.6.cloned.1.call-start = ((), (), s32[]{:S(2)}) async-start(), calls=%async_computation.10 | async-start | bytes 1310720 | tf_op jit(solution)/shard_map/all_gather | solution.py:1141
  11.4 23.1 %collective-permute-start.6 = (bf16[256,1024]{1,0:T(8,128)(2,1)S(1)}, bf16[256,1024]{1,0:T(8,128)(2,1)}, u32[]{:S(2)}, u32[]{:S(2)}) collective-permute-start(bf16[256,1024]{1,0:T(8,128)(2,1)S(1)} %get-tuple-element.102.refs_1_), channel_id=1, source_target_pairs={{0,68},{1,69},{2,70},{3,71},{4,64},{5,65},{6,66},{7,67},{8,76},{9,... | collective-permute-start | bytes 1572872 | tf_op jit(solution)/shard_map/ppermute | solution.py:38
  15.0 28.1 %all-to-all-start = ((bf16[8,32,1664]{2,1,0:T(8,128)(2,1)}), bf16[8,32,1664]{2,1,0:T(8,128)(2,1)S(1)}, u32[]{:S(2)}, u32[]{:S(2)}) async-start(bf16[8,32,1664]{2,1,0:T(8,128)(2,1)} %get-tuple-element.99), calls=%async_computation | async-start | bytes 1703936 | tf_op jit(solution)/shard_map/all_to_all | solution.py:753
  19.2 87.4 %all-gather.4.cloned.1.call-start = ((), (), s32[]{:S(2)}) async-start(), calls=%async_computation.7 | async-start | bytes 1179648 | tf_op jit(solution)/shard_map/all_gather | solution.py:1142
  36.2 15.5 %collective-permute-start.7 = (bf16[2,256,1024]{2,1,0:T(8,128)(2,1)S(1)}, bf16[2,256,1024]{2,1,0:T(8,128)(2,1)}, u32[]{:S(2)}, u32[]{:S(2)}) collective-permute-start(bf16[2,256,1024]{2,1,0:T(8,128)(2,1)S(1)} %fc2_hi.1.refs_1_), channel_id=1, source_target_pairs={{0,1},{1,2},{2,3},{3,0},{4,5},{5,6},{6,7},{7,4},{8,11},{9,8},{10,9... | collective-permute-start | bytes 3145736 | tf_op jit(solution)/shard_map/ppermute | solution.py:38
  40.9 20.1 %collective-permute-start.10 = (bf16[4,64,2048]{2,1,0:T(8,128)(2,1)}, bf16[4,64,2048]{2,1,0:T(8,128)(2,1)}, u32[]{:S(2)}, u32[]{:S(2)}) collective-permute-start(bf16[4,64,2048]{2,1,0:T(8,128)(2,1)} %bitcast.55), channel_id=1, source_target_pairs={{0,64},{1,65},{2,66},{3,67},{4,68},{5,69},{6,70},{7,71},{8,76},{9,... | collective-permute-start | bytes 3145736 | tf_op jit(solution)/shard_map/ppermute | solution.py:38
  43.1 13.8 %collective-permute-start.3 = (bf16[8,32,1664]{2,1,0:T(8,128)(2,1)S(1)}, bf16[8,32,1664]{2,1,0:T(8,128)(2,1)}, u32[]{:S(2)}, u32[]{:S(2)}) collective-permute-start(bf16[8,32,1664]{2,1,0:T(8,128)(2,1)S(1)} %all-to-all-done.refs_1_), channel_id=1, source_target_pairs={{0,16},{1,17},{2,18},{3,19},{4,20},{5,21},{6,22},{7,23},{8,56},{9,... | collective-permute-start | bytes 2555912 | tf_op jit(solution)/shard_map/ppermute | solution.py:38
  51.7 22.7 %collective-permute-start.8 = (bf16[2,256,1024]{2,1,0:T(8,128)(2,1)}, bf16[2,256,1024]{2,1,0:T(8,128)(2,1)}, u32[]{:S(2)}, u32[]{:S(2)}) collective-permute-start(bf16[2,256,1024]{2,1,0:T(8,128)(2,1)} %collective-permute-done.7.refs_2_), channel_id=1, source_target_pairs={{0,1},{1,2},{2,3},{3,0},{4,5},{5,6},{6,7},{7,4},{8,11},{9,8},{10,9... | collective-permute-start | bytes 3145736 | tf_op jit(solution)/shard_map/ppermute | solution.py:38
  55.2 13.5 %collective-permute-start = (bf16[384,1024]{1,0:T(8,128)(2,1)S(1)}, bf16[384,1024]{1,0:T(8,128)(2,1)}, u32[]{:S(2)}, u32[]{:S(2)}) collective-permute-start(bf16[384,1024]{1,0:T(8,128)(2,1)S(1)} %copy-done.22), channel_id=1, source_target_pairs={{0,8},{1,9},{2,10},{3,11},{4,12},{5,13},{6,14},{7,15},{8,0},{9,1},... | collective-permute-start | bytes 2359304 | tf_op jit(solution)/shard_map/ppermute | solution.py:38
  56.4 12.4 %collective-permute-start.1 = (bf16[384,1024]{1,0:T(8,128)(2,1)}, bf16[384,1024]{1,0:T(8,128)(2,1)}, u32[]{:S(2)}, u32[]{:S(2)}) collective-permute-start(bf16[384,1024]{1,0:T(8,128)(2,1)} %refs_7_.3), channel_id=1, source_target_pairs={{0,8},{1,9},{2,10},{3,11},{4,12},{5,13},{6,14},{7,15},{8,0},{9,1},... | collective-permute-start | bytes 2359304 | tf_op jit(solution)/shard_map/ppermute | solution.py:38
  56.6 136.5 %reduce-scatter.5.cloned.1.call-start = ((), (), s32[]{:S(2)}) async-start(), calls=%async_computation.9 | async-start | bytes 5242880 | tf_op jit(solution)/shard_map/reduce_scatter | solution.py:1226
  56.8 20.8 %collective-permute-start.4 = (bf16[8,32,1664]{2,1,0:T(8,128)(2,1)}, bf16[8,32,1664]{2,1,0:T(8,128)(2,1)}, u32[]{:S(2)}, u32[]{:S(2)}) collective-permute-start(bf16[8,32,1664]{2,1,0:T(8,128)(2,1)} %collective-permute-done.3.refs_2_), channel_id=1, source_target_pairs={{0,16},{1,17},{2,18},{3,19},{4,20},{5,21},{6,22},{7,23},{8,56},{9,... | collective-permute-start | bytes 2555912 | tf_op jit(solution)/shard_map/ppermute | solution.py:38
  61.0 17.4 %collective-permute-start.11 = (bf16[4,64,2048]{2,1,0:T(8,128)(2,1)}, bf16[4,64,2048]{2,1,0:T(8,128)(2,1)}, u32[]{:S(2)}, u32[]{:S(2)}) collective-permute-start(bf16[4,64,2048]{2,1,0:T(8,128)(2,1)} %collective-permute-done.10.refs_2_), channel_id=1, source_target_pairs={{0,64},{1,65},{2,66},{3,67},{4,68},{5,69},{6,70},{7,71},{8,76},{9,... | collective-permute-start | bytes 3145736 | tf_op jit(solution)/shard_map/ppermute | solution.py:38
  74.4 16.9 %collective-permute-start.9 = (bf16[2,256,1024]{2,1,0:T(8,128)(2,1)}, bf16[2,256,1024]{2,1,0:T(8,128)(2,1)S(1)}, u32[]{:S(2)}, u32[]{:S(2)}) collective-permute-start(bf16[2,256,1024]{2,1,0:T(8,128)(2,1)} %collective-permute-done.8.refs_3_), channel_id=1, source_target_pairs={{0,1},{1,2},{2,3},{3,0},{4,5},{5,6},{6,7},{7,4},{8,11},{9,8},{10,9... | collective-permute-start | bytes 3145736 | tf_op jit(solution)/shard_map/ppermute | solution.py:38
  77.6 12.1 %collective-permute-start.5 = (bf16[8,32,1664]{2,1,0:T(8,128)(2,1)}, bf16[8,32,1664]{2,1,0:T(8,128)(2,1)S(1)}, u32[]{:S(2)}, u32[]{:S(2)}) collective-permute-start(bf16[8,32,1664]{2,1,0:T(8,128)(2,1)} %collective-permute-done.4.refs_3_), channel_id=1, source_target_pairs={{0,16},{1,17},{2,18},{3,19},{4,20},{5,21},{6,22},{7,23},{8,56},{9,... | collective-permute-start | bytes 2555912 | tf_op jit(solution)/shard_map/ppermute | solution.py:38
  78.3 19.6 %collective-permute-start.12 = (bf16[4,64,2048]{2,1,0:T(8,128)(2,1)}, bf16[4,64,2048]{2,1,0:T(8,128)(2,1)S(1)}, u32[]{:S(2)}, u32[]{:S(2)}) collective-permute-start(bf16[4,64,2048]{2,1,0:T(8,128)(2,1)} %collective-permute-done.11.refs_3_), channel_id=1, source_target_pairs={{0,64},{1,65},{2,66},{3,67},{4,68},{5,69},{6,70},{7,71},{8,76},{9,... | collective-permute-start | bytes 3145736 | tf_op jit(solution)/shard_map/ppermute | solution.py:38
  129.9 106.1 %reduce-scatter.3.cloned.1.call-start = ((), (), s32[]{:S(2)}) async-start(), calls=%async_computation.8 | async-start | bytes 5242880 | tf_op jit(solution)/shard_map/reduce_scatter | solution.py:1258
  141.4 14.3 %collective-permute-start.14 = (bf16[640,1024]{1,0:T(8,128)(2,1)S(1)}, bf16[640,1024]{1,0:T(8,128)(2,1)S(1)}, u32[]{:S(2)}, u32[]{:S(2)}) collective-permute-start(bf16[640,1024]{1,0:T(8,128)(2,1)S(1)} %convolution_convert_fusion.refs_3_.refs_1_), channel_id=1, source_target_pairs={{0,8},{1,9},{2,10},{3,11},{4,12},{5,13},{6,14},{7,15},{8,0},{9,1},... | collective-permute-start | bytes 3932168 | tf_op jit(solution)/shard_map/ppermute | solution.py:38
  149.9 13.7 %collective-permute-start.15 = (bf16[4,64,1024]{2,1,0:T(8,128)(2,1)}, bf16[4,64,1024]{2,1,0:T(8,128)(2,1)S(1)}, u32[]{:S(2)}, u32[]{:S(2)}) collective-permute-start(bf16[4,64,1024]{2,1,0:T(8,128)(2,1)} %get-tuple-element.125), channel_id=1, source_target_pairs={{0,64},{1,65},{2,66},{3,67},{4,68},{5,69},{6,70},{7,71},{8,76},{9,... | collective-permute-start | bytes 1572872 | tf_op jit(solution)/shard_map/ppermute | solution.py:38
  163.9 13.7 %collective-permute-start.17 = (bf16[4,64,1024]{2,1,0:T(8,128)(2,1)S(1)}, bf16[4,64,1024]{2,1,0:T(8,128)(2,1)S(1)}, u32[]{:S(2)}, u32[]{:S(2)}) collective-permute-start(bf16[4,64,1024]{2,1,0:T(8,128)(2,1)S(1)} %get-tuple-element.132), channel_id=1, source_target_pairs={{0,64},{1,65},{2,66},{3,67},{4,68},{5,69},{6,70},{7,71},{8,76},{9,... | collective-permute-start | bytes 1572872 | tf_op jit(solution)/shard_map/ppermute | solution.py:38
  164.1 13.6 %collective-permute-start.18 = (bf16[2,128,1024]{2,1,0:T(8,128)(2,1)S(1)}, bf16[2,128,1024]{2,1,0:T(8,128)(2,1)S(1)}, u32[]{:S(2)}, u32[]{:S(2)}) collective-permute-start(bf16[2,128,1024]{2,1,0:T(8,128)(2,1)S(1)} %get-tuple-element.134), channel_id=1, source_target_pairs={{0,1},{1,2},{2,3},{3,0},{4,5},{5,6},{6,7},{7,4},{8,11},{9,8},{10,9... | collective-permute-start | bytes 1572872 | tf_op jit(solution)/shard_map/ppermute | solution.py:38
  184.4 12.1 %collective-permute-start.25 = (bf16[4,64,1024]{2,1,0:T(8,128)(2,1)}, bf16[4,64,1024]{2,1,0:T(8,128)(2,1)}, u32[]{:S(2)}, u32[]{:S(2)}) collective-permute-start(bf16[4,64,1024]{2,1,0:T(8,128)(2,1)} %get-tuple-element.156), channel_id=1, source_target_pairs={{0,64},{1,65},{2,66},{3,67},{4,68},{5,69},{6,70},{7,71},{8,76},{9,... | collective-permute-start | bytes 1572872 | tf_op jit(solution)/shard_map/ppermute | solution.py:38
  184.6 11.9 %collective-permute-start.26 = (bf16[2,128,1024]{2,1,0:T(8,128)(2,1)}, bf16[2,128,1024]{2,1,0:T(8,128)(2,1)}, u32[]{:S(2)}, u32[]{:S(2)}) collective-permute-start(bf16[2,128,1024]{2,1,0:T(8,128)(2,1)} %get-tuple-element.158), channel_id=1, source_target_pairs={{0,1},{1,2},{2,3},{3,0},{4,5},{5,6},{6,7},{7,4},{8,11},{9,8},{10,9... | collective-permute-start | bytes 1572872 | tf_op jit(solution)/shard_map/ppermute | solution.py:38
  190.1 35.0 %collective-permute-start.20 = (bf16[320,1024]{1,0:T(8,128)(2,1)}, bf16[320,1024]{1,0:T(8,128)(2,1)}, u32[]{:S(2)}, u32[]{:S(2)}) collective-permute-start(bf16[320,1024]{1,0:T(8,128)(2,1)} %convolution_convert_fusion.2), channel_id=1, source_target_pairs={{0,8},{1,9},{2,10},{3,11},{4,12},{5,13},{6,14},{7,15},{8,0},{9,1},... | collective-permute-start | bytes 1966088 | tf_op jit(solution)/shard_map/ppermute | solution.py:38
  193.0 39.9 %collective-permute-start.19 = (bf16[320,1024]{1,0:T(8,128)(2,1)}, bf16[320,1024]{1,0:T(8,128)(2,1)}, u32[]{:S(2)}, u32[]{:S(2)}) collective-permute-start(bf16[320,1024]{1,0:T(8,128)(2,1)} %convolution_convert_fusion.4), channel_id=1, source_target_pairs={{0,8},{1,9},{2,10},{3,11},{4,12},{5,13},{6,14},{7,15},{8,0},{9,1},... | collective-permute-start | bytes 1966088 | tf_op jit(solution)/shard_map/ppermute | solution.py:38
  201.7 14.7 %all-to-all-start.1 = ((bf16[4,64,1024]{2,1,0:T(8,128)(2,1)}), bf16[4,64,1024]{2,1,0:T(8,128)(2,1)S(1)}, u32[]{:S(2)}, u32[]{:S(2)}) async-start(bf16[4,64,1024]{2,1,0:T(8,128)(2,1)} %copy-done.33), calls=%async_computation.3 | async-start | bytes 1048576 | tf_op jit(solution)/shard_map/all_to_all | solution.py:753
  210.9 18.0 %collective-permute-start.21 = (bf16[2,64,1024]{2,1,0:T(8,128)(2,1)}, bf16[2,64,1024]{2,1,0:T(8,128)(2,1)}, u32[]{:S(2)}, u32[]{:S(2)}) collective-permute-start(bf16[2,64,1024]{2,1,0:T(8,128)(2,1)} %get-tuple-element.150), channel_id=1, source_target_pairs={{0,1},{1,2},{2,3},{3,0},{4,5},{5,6},{6,7},{7,4},{8,9},{9,10},{10,1... | collective-permute-start | bytes 786440 | tf_op jit(solution)/shard_map/ppermute | solution.py:38
  212.2 16.6 %collective-permute-start.22 = (bf16[2,64,1024]{2,1,0:T(8,128)(2,1)}, bf16[2,64,1024]{2,1,0:T(8,128)(2,1)}, u32[]{:S(2)}, u32[]{:S(2)}) collective-permute-start(bf16[2,64,1024]{2,1,0:T(8,128)(2,1)} %get-tuple-element.151), channel_id=1, source_target_pairs={{0,2},{1,3},{2,0},{3,1},{4,6},{5,7},{6,4},{7,5},{8,10},{9,11},{10,... | collective-permute-start | bytes 786440 | tf_op jit(solution)/shard_map/ppermute | solution.py:38
  214.6 14.2 %collective-permute-start.23 = (bf16[2,64,1024]{2,1,0:T(8,128)(2,1)}, bf16[2,64,1024]{2,1,0:T(8,128)(2,1)}, u32[]{:S(2)}, u32[]{:S(2)}) collective-permute-start(bf16[2,64,1024]{2,1,0:T(8,128)(2,1)} %get-tuple-element.152), channel_id=1, source_target_pairs={{0,3},{1,0},{2,1},{3,2},{4,7},{5,4},{6,5},{7,6},{8,11},{9,8},{10,9... | collective-permute-start | bytes 786440 | tf_op jit(solution)/shard_map/ppermute | solution.py:38
  217.8 18.2 %all-to-all-start.2 = ((bf16[8,16,2048]{2,1,0:T(8,128)(2,1)}), bf16[8,16,2048]{2,1,0:T(8,128)(2,1)S(1)}, u32[]{:S(2)}, u32[]{:S(2)}) async-start(bf16[8,16,2048]{2,1,0:T(8,128)(2,1)} %fc1_slices.1), calls=%async_computation.4 | async-start | bytes 1048576 | tf_op jit(solution)/shard_map/all_to_all | solution.py:753
  239.1 22.9 %all-to-all-start.3 = ((bf16[8,32,2176]{2,1,0:T(8,128)(2,1)}), bf16[8,32,2176]{2,1,0:T(8,128)(2,1)S(1)}, u32[]{:S(2)}, u32[]{:S(2)}) async-start(bf16[8,32,2176]{2,1,0:T(8,128)(2,1)} %join.1), calls=%async_computation.5 | async-start | bytes 2228224 | tf_op jit(solution)/shard_map/all_to_all | solution.py:753
  244.0 19.1 %collective-permute-start.29 = (bf16[32,1024]{1,0:T(8,128)(2,1)S(1)}, bf16[32,1024]{1,0:T(8,128)(2,1)S(1)}, u32[]{:S(2)}, u32[]{:S(2)}) collective-permute-start(bf16[32,1024]{1,0:T(8,128)(2,1)S(1)} %get-tuple-element.166), channel_id=1, source_target_pairs={{0,64},{1,65},{2,66},{3,67},{4,68},{5,69},{6,70},{7,71},{8,72},{9,... | collective-permute-start | bytes 196616 | tf_op jit(solution)/shard_map/ppermute | solution.py:38
  (70 other events, 585.2 us)
Sparse Core Ops, SparseCore 0:
  11.5 29.3 all-gather.5
  130.1 46.0 reduce-scatter.4
  184.5 49.2 reduce-scatter.2
Sparse Core Ops, SparseCore 1:
  56.6 47.9 all-gather.3
